TPU v7x, 256 devices: a whole 4x4x8 slice. The times are simulated.
256 devices in a mesh: blk: 16 (over z, core), head: 8 (over x, y_lo), cfg: 2 (over y_hi).
Axes of the slice: x: 4, y: 4 (y_hi: 2, y_lo: 2; y = y_hi * 2 + y_lo), z: 8, core: 2. Of those that a mesh axis runs over, the one named last changes fastest.
Arguments:
- fresh: bfloat16 [8192, 3, 5120], P(('cfg', 'blk', 'head')), parts along dimension 0, may hold values from -96 to 96, as said below
- rows_index: int32 [4096], P('blk'), may hold values from 0 to 511, as said below
- counts: int32 [16], replicated, may hold values from 64 to 256, as said below
- key_cache: bfloat16 [16384, 5120], P(('cfg', 'blk'), 'head'), parts along dimension 0, may hold values from -6 to 6
- value_cache: bfloat16 [16384, 5120], P(('cfg', 'blk'), 'head'), parts along dimension 0, may hold values from -48 to 48
- q_gain: bfloat16 [5120], replicated, may hold values from 0.099609375 to 1.8984375
- k_gain: bfloat16 [5120], replicated, may hold values from 0.099609375 to 1.8984375
- out_weight: bfloat16 [5120, 5120], P('head'), may hold values from -0.25 to 0.25
Outputs:
- mixed: bfloat16 [8192, 5120], P(('cfg', 'blk', 'head')), parts along dimension 0
There are 2 independent parts, one for each index of `cfg`. A program takes and returns all parts, laid end to end along the dimension named above; an argument that names none is the same for every part. Nothing has to cross between parts.
Inputs may be any that keep to these rules, and one draw needn't show every extreme that they name: `rows_index`: within each shard's 256 slots the values are distinct positions of that shard. counts[j] live slots of shard j are its first slots; the counts sum to exactly 2048, and some shard has all 256 slots live; the counts of the shards before shard j sum to more than j * 128 - 3 * 64 and less than j * 128 + 3 * 64. `fresh`: slots that are not live carry data that no output reads.
All inputs are finite; a program needn't handle non-finite values.
Results may differ from a plain program's by a relative error of at most 0.035.
Values may be sent and summed in bfloat16 or wider, within the bound.
A program may use at most 128 MiB of HBM per device.

v0:
```python
import math

import jax
import jax.numpy as jnp
from jax import lax
from jax.sharding import PartitionSpec as P

HEAD_DIM = 128


EPS = 1e-06
NEG = -1e30


def normalize(rows, gains):
    values = rows.astype(jnp.float32)
    mean_sq = jnp.mean(values * values, axis=-1, keepdims=True)
    return (values * lax.rsqrt(mean_sq + EPS) * gains.astype(jnp.float32)).astype(jnp.bfloat16)


def absorb(queries, running, keys, values):
    highest, totals, weighted = running
    scale = 1.0 / math.sqrt(HEAD_DIM)
    scores = jnp.einsum("rhe,nhe->rhn", queries, keys, preferred_element_type=jnp.float32) * scale
    new_max = jnp.maximum(highest, jnp.max(scores, axis=-1))
    factor = jnp.exp(highest - new_max)
    weights = jnp.exp(scores - new_max[..., None])
    totals = totals * factor + jnp.sum(weights, axis=-1)
    weighted = weighted * factor[..., None] + jnp.einsum(
        "rhn,nhe->rhe", weights.astype(jnp.bfloat16), values, preferred_element_type=jnp.float32
    )
    return (new_max, totals, weighted)


def absorb_blocks(queries, running, keys, values):
    key_count = keys.shape[0]
    tile_len = 512
    head_count = queries.shape[1]
    key_tiles = keys.reshape(key_count // tile_len, tile_len, head_count, HEAD_DIM)
    value_tiles = values.reshape(key_count // tile_len, tile_len, head_count, HEAD_DIM)

    def absorb_tile(state_now, tile_pair):
        return (absorb(queries, state_now, tile_pair[0], tile_pair[1]), None)

    running, _ = lax.scan(absorb_tile, running, (key_tiles, value_tiles))
    return running


def empty_state(row_total, head_count):
    return (
        jnp.full((row_total, head_count), NEG, jnp.float32),
        jnp.zeros((row_total, head_count), jnp.float32),
        jnp.zeros((row_total, head_count, HEAD_DIM), jnp.float32),
    )


def attend(query_rows, keys, values):
    row_total = query_rows.shape[0]
    head_count = query_rows.shape[1] // HEAD_DIM
    shaped = query_rows.reshape(row_total, head_count, HEAD_DIM)
    keys = keys.reshape(keys.shape[0], head_count, HEAD_DIM)
    values = values.reshape(values.shape[0], head_count, HEAD_DIM)
    start_state = empty_state(row_total, head_count)
    final_state = absorb_blocks(
        shaped,
        start_state,
        lax.all_gather(keys, "blk", axis=0, tiled=True),
        lax.all_gather(values, "blk", axis=0, tiled=True),
    )
    _, totals, weighted = final_state
    return (
        (weighted / totals[..., None])
        .reshape(row_total, head_count * HEAD_DIM)
        .astype(jnp.bfloat16)
    )


def local(fresh, rows_index, counts, key_cache, value_cache, q_gain, k_gain, out_weight):
    group_size = lax.axis_size("head")
    local_rows = fresh.shape[0]
    width = fresh.shape[2]
    normed_q = normalize(fresh[:, 0], q_gain)
    normed_k = normalize(fresh[:, 1], k_gain)
    packed = jnp.stack([normed_q, normed_k, fresh[:, 2]], axis=1).reshape(
        local_rows, 3, group_size, width // group_size
    )
    by_heads = lax.all_to_all(packed, "head", split_axis=2, concat_axis=0, tiled=True)
    capacity = local_rows * group_size
    group_width = width // group_size
    by_heads = by_heads.reshape(capacity, 3, group_width)
    fresh_q = by_heads[:, 0]
    fresh_k = by_heads[:, 1]
    fresh_v = by_heads[:, 2]
    position = lax.axis_index("blk")
    live_count = jnp.take(counts, position)
    slot_ids = jnp.arange(capacity, dtype=jnp.int32)
    is_live = slot_ids < live_count
    targets = jnp.where(is_live, rows_index, key_cache.shape[0])
    keys = key_cache.at[targets].set(fresh_k, mode="drop")
    values = value_cache.at[targets].set(fresh_v, mode="drop")
    attention = attend(fresh_q, keys, values)
    attention = jnp.where(is_live[:, None], attention, jnp.zeros((), jnp.bfloat16))
    return lax.psum_scatter(
        jnp.dot(attention, out_weight, preferred_element_type=jnp.float32).astype(jnp.bfloat16),
        "head",
        scatter_dimension=0,
        tiled=True,
    )


def solution(mesh):
    placed = (
        P(("cfg", "blk", "head"), None, None),
        P("blk"),
        P(),
        P(("cfg", "blk"), "head"),
        P(("cfg", "blk"), "head"),
        P(),
        P(),
        P("head", None),
    )
    return jax.shard_map(
        local,
        mesh=mesh,
        in_specs=placed,
        out_specs=P(("cfg", "blk", "head"), None),
        check_vma=False,
    )
```

profile of v0, /device:TPU:8, one launch (start us, length us, event | category | flops | bytes accessed | tf_op | source)
XLA Modules:
  0.0 319.4 jit_solution(7375154343041475149)
XLA Ops:
  9.7 5.8 %all-to-all-start = ((bf16[32,3,8,640]{3,0,1,2:T(8,128)(2,1)}), bf16[32,3,8,640]{3,0,1,2:T(8,128)(2,1)S(1)}, u32[]{:S(2)}, u32[]{:S(2)}) async-start(bf16[32,3,8,640]{3,0,1,2:T(8,128)(2,1)} %copy.44), calls=%async_computation | async-start | bytes 1966080 | tf_op jit(solution)/shard_map/all_to_all | solution.py:87
  16.7 12.6 %all-to-all-done = bf16[32,3,8,640]{3,0,1,2:T(8,128)(2,1)S(1)} async-done(((bf16[32,3,8,640]{3,0,1,2:T(8,128)(2,1)}), bf16[32,3,8,640]{3,0,1,2:T(8,128)(2,1)S(1)}, u32[]{:S(2)}, u32[]{:S(2)}) %all-to-all-start) | async-done | bytes 983072 | tf_op jit(solution)/shard_map/all_to_all | solution.py:87
  29.4 2.0 scatter_custom_fusion
  32.6 2.0 scatter_custom_fusion.1
  36.3 63.3 %all-gather.3.cloned.1.call-done = bf16[8192,5,128]{0,2,1:T(8,128)(2,1)} async-done(((bf16[512,5,128]{0,2,1:T(8,128)(2,1)}), bf16[8192,5,128]{0,2,1:T(8,128)(2,1)}) %all-gather.3.cloned.1.call-update) | async-done | bytes 10485776 | tf_op jit(solution)/shard_map/all_gather | solution.py:67
  99.6 14.2 %copy.47 = bf16[8192,5,128]{2,0,1:T(8,128)(2,1)} copy(bf16[8192,5,128]{0,2,1:T(8,128)(2,1)} %all-gather.3.cloned.1.call-done) | data formatting | bytes 20971520 | tf_op jit(solution)/shard_map/all_gather | solution.py:67
  113.8 52.0 %all-gather.5.cloned.1.call-done = bf16[8192,5,128]{0,2,1:T(8,128)(2,1)} async-done(((bf16[512,5,128]{0,2,1:T(8,128)(2,1)}), bf16[8192,5,128]{0,2,1:T(8,128)(2,1)}) %all-gather.5.cloned.1.call-update) | async-done | bytes 10485776 | tf_op jit(solution)/shard_map/all_gather | solution.py:68
  165.8 14.2 %copy.50 = bf16[8192,5,128]{2,0,1:T(8,128)(2,1)} copy(bf16[8192,5,128]{0,2,1:T(8,128)(2,1)} %all-gather.5.cloned.1.call-done) | data formatting | bytes 20971520 | tf_op jit(solution)/shard_map/all_gather | solution.py:68
  180.0 64.5 %while.16 = (s32[]{:T(128)}, f32[256,5]{0,1:T(8,128)S(1)}, f32[256,5]{0,1:T(8,128)S(1)}, f32[256,5,128]{0,2,1:T(8,128)S(1)}, bf16[16,512,5,128]{3,1,0,2:T(8,128)...) while((s32[]{:T(128)}, f32[256,5]{0,1:T(8,128)S(1)}, ...), condition=%wide.region_7.8_spmd.clone, body=%wide.region_4.7_spmd.clone.sunk | while | flops 341285120 | bytes 10895481 | solution.py:45
  182.1 1.9 fusion.44
  186.1 1.9 fusion.44
  190.1 1.9 fusion.44
  194.2 1.9 fusion.44
  198.2 1.9 fusion.44
  202.2 1.9 fusion.44
  206.3 1.9 fusion.44
  210.3 1.9 fusion.44
  218.4 1.9 fusion.44
  222.4 1.9 fusion.44
  230.5 1.9 fusion.44
  234.5 1.9 fusion.44
  242.6 1.9 fusion.44
  244.6 6.6 %convolution_convert_fusion = bf16[256,5120]{1,0:T(8,128)(2,1)} fusion(bf16[256,640]{0,1:T(8,128)(2,1)S(1)} %bitcast_select_fusion, bf16[640,5120]{1,0:T(8,128)(2,1)} %param.17), kind=kOutput, calls=%fused_computation.25 | convolution fusion | flops 1679032320 | bytes 9502720 | tf_op jit(solution)/shard_map/dot_general | solution.py:104
  251.3 61.6 %reduce-scatter.2.cloned.1.call-done = bf16[32,5120]{1,0:T(8,128)(2,1)} async-done(((bf16[256,5120]{1,0:T(8,128)(2,1)}), bf16[32,5120]{1,0:T(8,128)(2,1)}) %reduce-scatter.2.cloned.1.call-update) | async-done | bytes 327696 | tf_op jit(solution)/shard_map/reduce_scatter | solution.py:103
  (129 shorter events, 45.4 us)
Async XLA Ops:
  6.5 1.2 copy-start
  6.5 1.5 slice-start
  6.5 1.5 copy-start.3
  6.5 1.5 copy-start.4
  8.4 7.0 %copy-start.6 = (s32[16]{0:T(128)S(1)}, s32[16]{0:T(128)}, u32[]{:S(2)}) copy-start(s32[16]{0:T(128)} %param.12) | copy-start | bytes 196
  8.5 8.2 %copy-start.5 = (s32[256]{0:T(256)S(1)}, s32[256]{0:T(256)}, u32[]{:S(2)}) copy-start(s32[256]{0:T(256)} %param.11) | copy-start | bytes 3076
  8.6 20.8 %copy-start.2 = (bf16[512,640]{1,0:T(8,128)(2,1)S(1)}, bf16[512,640]{1,0:T(8,128)(2,1)}, u32[]{:S(2)}) copy-start(bf16[512,640]{1,0:T(8,128)(2,1)} %param.13) | copy-start | bytes 1966084
  9.7 19.6 %all-to-all-start = ((bf16[32,3,8,640]{3,0,1,2:T(8,128)(2,1)}), bf16[32,3,8,640]{3,0,1,2:T(8,128)(2,1)S(1)}, u32[]{:S(2)}, u32[]{:S(2)}) async-start(bf16[32,3,8,640]{3,0,1,2:T(8,128)(2,1)} %copy.44), calls=%async_computation | async-start | bytes 1966080 | tf_op jit(solution)/shard_map/all_to_all | solution.py:87
  15.4 17.2 %copy-start.1 = (bf16[512,640]{1,0:T(8,128)(2,1)S(1)}, bf16[512,640]{1,0:T(8,128)(2,1)}, u32[]{:S(2)}) copy-start(bf16[512,640]{1,0:T(8,128)(2,1)} %param.14) | copy-start | bytes 1966084
  15.4 84.1 %all-gather.3.cloned.1.call-start = ((), (), s32[]{:S(2)}) async-start(), calls=%async_computation.2 | async-start | bytes 11141120 | tf_op jit(solution)/shard_map/all_gather | solution.py:67
  32.6 133.2 %all-gather.5.cloned.1.call-start = ((), (), s32[]{:S(2)}) async-start(), calls=%async_computation.3 | async-start | bytes 11141120 | tf_op jit(solution)/shard_map/all_gather | solution.py:68
  35.7 277.1 %reduce-scatter.2.cloned.1.call-start = ((), (), s32[]{:S(2)}) async-start(), calls=%async_computation.4 | async-start | bytes 2949120 | tf_op jit(solution)/shard_map/reduce_scatter | solution.py:103
Sparse Core Ops, SparseCore 0:
  32.7 66.8 all-gather.2
  101.4 64.3 all-gather.4
  251.4 61.4 reduce-scatter.1
where the time goes:
time: 323 us; the launch traced here: 319 us
  waiting for transfers between devices  190 us (59%)
  matrix products  62.8 us (19%)
  local copies, waits for them, and re-layouts  38.1 us (12%)
  between operations  14 us (4%)
  other arithmetic  8.06 us (2%)
  starting transfers between devices  5.84 us (2%)
    all_gather x1, waiting for transfers between devices, attend(): lax.all_gather(keys, 'blk', axis=0, tiled=True)  63.3 us
    reduce_scatter x1, waiting for transfers between devices, local(): lax.psum_scatter(jnp.dot(attention, out_weight, preferred_element_type=jn...  61.6 us
    all_gather x1, waiting for transfers between devices, attend(): lax.all_gather(values, 'blk', axis=0, tiled=True)  52 us
    dot_general x16, matrix products, absorb(): jnp.einsum('rhn,nhe->rhe', weights.astype(jnp.bfloat16), values, preferre...  30.5 us
    dot_general x16, matrix products, absorb(): jnp.einsum('rhe,nhe->rhn', queries, keys, preferred_element_type=jnp.floa...  25.7 us
    all_gather x1, local copies, waits for them, and re-layouts, attend(): lax.all_gather(keys, 'blk', axis=0, tiled=True)  14.2 us
    all_gather x1, local copies, waits for them, and re-layouts, attend(): lax.all_gather(values, 'blk', axis=0, tiled=True)  14.2 us
    all_to_all x1, waiting for transfers between devices, local(): lax.all_to_all(packed, 'head', split_axis=2, concat_axis=0, tiled=True)  12.6 us
  transfers between devices with their start and end apart: 4, of which 4 were waited for; matrix products, arithmetic and copies ran while one was open for 6% of the time, Pallas kernels for 0%

commit v1 on v0

v1 whole, which is shorter than its diff:
```python
import functools
import math

import jax
import jax.numpy as jnp
from jax import lax
from jax.experimental import pallas as pl
from jax.experimental.pallas import tpu as pltpu
from jax.sharding import PartitionSpec as P

HEAD_DIM = 128
EPS = 1e-06
MESH = pl.DeviceIdType.MESH
BF = jnp.bfloat16
F32 = jnp.float32

D = 5120
GROUP = 640
NH = GROUP // HEAD_DIM
NG = 8
NB = 16
CAP = 256
L_BLK = 512
ROWS = 32
CH = 128
SPAN = 512
BASE = 192
PART = ((0, 3), (3, 5))
C1 = 3072
C1H = C1 // 2
C2 = D - C1
C2H = C2 // 2
SCALE2 = math.log2(math.e) / math.sqrt(HEAD_DIM)


def nt(a, b):
    return lax.dot_general(a, b, (((1,), (1,)), ((), ())), preferred_element_type=F32)


def mm(a, b):
    return jnp.dot(a, b, preferred_element_type=F32)


def kernel(
    fresh, ridx, counts, kcache, vcache, qgain, kgain, weight, out,
    fv, gq, gk, kc, vc, wv, sent, got, selq, rbuf, kfull, vt, qs,
    of, st, so, ss, ro, rs, abuf, cat, att, pb,
    rx1, ac1, ry1, sy1, ry2, sx2, rx2, ac2,
    lsem, asend, arecv, rsend, rrecv, ksend, krecv, gsend, grecv,
    dsend, drecv, tsend, trecv, usend, urecv, esend, erecv,
):
    j = lax.axis_index("blk")
    h = lax.axis_index("head")
    core = lax.rem(j, 2)
    x, y = lax.div(h, 2), lax.rem(h, 2)
    pending = []

    def blk_at(offset):
        return {"blk": lax.rem(j + offset + NB, NB)}

    sibling = {"blk": j + 1 - 2 * core}

    def head_at(dx, dy):
        other_y = 1 - y if dy else y
        return lax.rem(x + dx, 4) * 2 + other_y

    def send(src, dst, s, r, dev):
        copy = pltpu.make_async_remote_copy(
            src_ref=src, dst_ref=dst, send_sem=s, recv_sem=r, device_id=dev, device_id_type=MESH
        )
        copy.start()
        pending.append(copy)
        return copy

    loads = [
        pltpu.make_async_copy(src, dst, lsem.at[i])
        for i, (src, dst) in enumerate((
            (fresh.at[0], fv.at[0]), (qgain, gq), (fresh.at[1], fv.at[1]), (kgain, gk),
            (fresh.at[2], fv.at[2]), (kcache, kc), (vcache, vc), (weight, wv),
        ))
    ]
    for load in loads:
        load.start()

    barrier = pltpu.get_barrier_semaphore()
    pairs = [(dx, dy) for dx in range(4) for dy in range(2) if dx or dy]
    for dx, dy in pairs:
        pl.semaphore_signal(barrier, inc=1, device_id={"head": head_at(dx, dy)}, device_id_type=MESH)
    for offset in (-2, -1, 1, 2):
        pl.semaphore_signal(barrier, inc=1, device_id=blk_at(offset), device_id_type=MESH)
    pl.semaphore_wait(barrier, len(pairs) + 4)

    live = counts[j]
    before = jnp.int32(0)
    for i in range(NB):
        before = before + jnp.where(i < j, counts[i], 0)
    shift = before - CH * j + BASE

    my_rows = pl.ds(pl.multiple_of(h * ROWS, ROWS), ROWS)
    a_copies = [[], [], []]
    for t in range(3):
        loads[2 * t].wait()
        if t < 2:
            loads[2 * t + 1].wait()
            rows = fv[t].astype(F32)
            mean_sq = jnp.mean(rows * rows, axis=-1, keepdims=True)
            gains = (gq if t == 0 else gk)[...].astype(F32)
            rows = (rows * lax.rsqrt(mean_sq + EPS) * gains).astype(BF)
        else:
            rows = fv[2]
        for g in range(NG):
            sent[t, g] = rows[:, g * GROUP:(g + 1) * GROUP]
        for n, (dx, dy) in enumerate(pairs):
            peer = head_at(dx, dy)
            a_copies[t].append(send(
                sent.at[t, peer], got.at[t, my_rows], asend.at[t, n], arecv.at[t, n], {"head": peer}
            ))
        got[t, my_rows] = sent[t, h]

    for copy in a_copies[0]:
        copy.wait_recv()
    r_id = lax.broadcasted_iota(jnp.int32, (SPAN, CAP), 0)
    s_id = lax.broadcasted_iota(jnp.int32, (SPAN, CAP), 1)
    place = ((r_id - s_id) == shift) & (s_id < live)
    selq[...] = mm(place.astype(F32).astype(BF), got[0]).astype(BF)
    r_copies = [
        send(selq.at[pl.ds(first, size)], rbuf.at[pl.ds(to, size)], rsend.at[n], rrecv.at[n], blk_at(offset))
        for n, (first, size, to, offset) in enumerate(
            ((64, 128, 0, -1), (320, 128, 128, 1), (0, 64, 256, -2), (448, 64, 320, 2))
        )
    ]
    for copy in r_copies:
        copy.wait_recv()
    mine = (selq[192:320].astype(F32) + rbuf[0:128].astype(F32)) + rbuf[128:256].astype(F32)
    qs[0, 0:64] = (mine[0:64] + rbuf[320:384].astype(F32)).astype(BF)
    qs[0, 64:128] = (mine[64:128] + rbuf[256:320].astype(F32)).astype(BF)

    halves = (pl.ds(0, 64), pl.ds(64, 64))

    def gather_step(step):
        copies = []
        for half in range(2):
            for way in range(2):
                if step == 4 and half != way:
                    continue
                src = (8 - (step - 1)) % 8 if way == 0 else step - 1
                dst = 8 - step if way == 0 else step
                copies.append(send(
                    qs.at[src, halves[half]], qs.at[dst, halves[half]],
                    gsend.at[way, step - 1, half], grecv.at[way, step - 1, half],
                    blk_at(2 if way == 0 else -2),
                ))
        return copies

    g_copies = gather_step(1)

    for t in (1, 2):
        for copy in a_copies[t]:
            copy.wait_recv()
    loads[5].wait()
    loads[6].wait()
    pos = lax.broadcasted_iota(jnp.int32, (L_BLK, CAP), 0)
    slot = lax.broadcasted_iota(jnp.int32, (L_BLK, CAP), 1)
    hits = ((pos == ridx[...]) & (slot < live)).astype(F32)
    hit = jnp.sum(hits, axis=1, keepdims=True) > 0.5
    hits = hits.astype(BF)
    kfull[0] = jnp.where(hit, mm(hits, got[1]), kc[...].astype(F32)).astype(BF)
    k_copy = send(kfull.at[0], kfull.at[1], ksend.at[0], krecv.at[0], sibling)
    vt[0] = jnp.where(hit, mm(hits, got[2]), vc[...].astype(F32)).T.astype(BF)
    v_copy = send(vt.at[0], vt.at[1], ksend.at[1], krecv.at[1], sibling)

    def attend(slots):
        width = CH * len(slots)
        for i in range(NH):
            cols = slice(i * HEAD_DIM, (i + 1) * HEAD_DIM)
            if len(slots) == 1:
                query = qs[slots[0], :, cols]
            else:
                query = jnp.concatenate([qs[s, :, cols] for s in slots], axis=0)
            s0 = nt(kfull[0, :, cols], query)
            s1 = nt(kfull[1, :, cols], query)
            top = jnp.maximum(jnp.max(s0, axis=0, keepdims=True), jnp.max(s1, axis=0, keepdims=True)) * SCALE2
            p0 = jnp.exp2(s0 * SCALE2 - top)
            p1 = jnp.exp2(s1 * SCALE2 - top)
            total = jnp.sum(p0, axis=0, keepdims=True) + jnp.sum(p1, axis=0, keepdims=True)
            o = mm(vt[0, cols, :], p0.astype(BF)) + mm(vt[1, cols, :], p1.astype(BF))
            part, row = (0, i) if i < 3 else (1, i - 3)
            for n, s in enumerate(slots):
                lanes = slice(n * CH, (n + 1) * CH)
                of[s, cols, :] = o[:, lanes]
                st[s, part, row:row + 1, :] = top[:, lanes]
                st[s, part, 8 + row:9 + row, :] = total[:, lanes]

    st[...] = jnp.zeros_like(st)
    for copy in g_copies:
        copy.wait_recv()
    g_copies = gather_step(2)
    k_copy.wait_recv()
    v_copy.wait_recv()
    attend((7, 1))
    for copy in g_copies:
        copy.wait_recv()
    g_copies = gather_step(3)
    attend((6, 2))
    for copy in g_copies:
        copy.wait_recv()
    g_copies = gather_step(4)
    attend((5, 3))
    for copy in g_copies:
        copy.wait_recv()
    attend((4,))

    def part_rows(part):
        first, last = PART[part]
        return pl.ds(first * HEAD_DIM, (last - first) * HEAD_DIM)

    def joined(slot, part, arrivals):
        first, last = PART[part]
        tops = [st[slot, part, 0:8]] + [rs[way, step, part, 0:8] for way, step in arrivals]
        sums = [st[slot, part, 8:16]] + [rs[way, step, part, 8:16] for way, step in arrivals]
        top = functools.reduce(jnp.maximum, tops)
        factors = [jnp.exp2(t - top) for t in tops]
        total = sum(a * f for a, f in zip(sums, factors))
        values = []
        for i in range(first, last):
            rows = slice(i * HEAD_DIM, (i + 1) * HEAD_DIM)
            k = i - first
            value = of[slot, rows, :] * factors[0][k:k + 1]
            for n, (way, step) in enumerate(arrivals):
                value = value + ro[way, step, rows, :].astype(F32) * factors[n + 1][k:k + 1]
            values.append(value)
        return values, top, total

    d_copies = {}

    def give(way, step, part):
        ahead = 5 - step
        slot = ahead if way == 0 else 8 - ahead
        first_step = 1 if part == way else 2
        if step > first_step:
            for copy in d_copies[way, step - 1, part]:
                copy.wait_recv()
            values, top, total = joined(slot, part, [(way, step - 2)])
        else:
            first, last = PART[part]
            values = [of[slot, i * HEAD_DIM:(i + 1) * HEAD_DIM, :] for i in range(first, last)]
            top, total = st[slot, part, 0:8], st[slot, part, 8:16]
        for n, value in enumerate(values):
            i = PART[part][0] + n
            so[way, step - 1, i * HEAD_DIM:(i + 1) * HEAD_DIM, :] = value.astype(BF)
        ss[way, step - 1, part, 0:8] = top
        ss[way, step - 1, part, 8:16] = total
        rows = part_rows(part)
        dev = blk_at(2 if way == 0 else -2)
        d_copies[way, step, part] = [
            send(ss.at[way, step - 1, part], rs.at[way, step - 1, part],
                 tsend.at[way, step - 1, part], trecv.at[way, step - 1, part], dev),
            send(so.at[way, step - 1, rows], ro.at[way, step - 1, rows],
                 dsend.at[way, step - 1, part], drecv.at[way, step - 1, part], dev),
        ]

    give(0, 1, 0)
    give(1, 1, 1)
    give(0, 2, 1)
    give(1, 2, 0)
    attend((0,))
    give(0, 2, 0)
    give(1, 2, 1)
    for step in (3, 4):
        give(0, step, 1)
        give(1, step, 0)
        give(0, step, 0)
        give(1, step, 1)
    for part in (1, 0):
        for way in range(2):
            for copy in d_copies[way, 4, part]:
                copy.wait_recv()
        values, _, total = joined(0, part, [(0, 3), (1, 3)])
        for n, value in enumerate(values):
            i = PART[part][0] + n
            result = (value / total[n:n + 1]).T.astype(BF)
            abuf[:, i * HEAD_DIM:(i + 1) * HEAD_DIM] = result

    u_copies = [
        send(abuf.at[pl.ds(first, size)], cat.at[pl.ds(to, size)], usend.at[n], urecv.at[n], blk_at(offset))
        for n, (first, size, to, offset) in enumerate(
            ((0, 128, 320, -1), (0, 128, 64, 1), (0, 64, 448, -2), (64, 64, 0, 2))
        )
    ]
    cat[192:320] = abuf[...]
    r_id = lax.broadcasted_iota(jnp.int32, (CAP, SPAN), 1)
    s_id = lax.broadcasted_iota(jnp.int32, (CAP, SPAN), 0)
    place = (((r_id - s_id) == shift) & (s_id < live)).astype(F32).astype(BF)
    for copy in u_copies:
        copy.wait_recv()
    att[...] = mm(place, cat[...]).astype(BF)

    loads[7].wait()

    def project(first, last):
        @pl.loop(first // 256, last // 256)
        def _(i):
            cols = pl.ds(pl.multiple_of(i * 256, 256), 256)
            tile = mm(att[...], wv[:, cols]).astype(BF)
            for g in range(NG):
                pb[g // 2, g % 2, :, cols] = tile[g * ROWS:(g + 1) * ROWS]

    up, down, far = lax.rem(x + 1, 4), lax.rem(x + 3, 4), lax.rem(x + 2, 4)
    to_up, to_down = {"head": up * 2 + y}, {"head": down * 2 + y}
    to_pair = {"head": x * 2 + 1 - y}
    a1, b1 = pl.ds(0, C1H), pl.ds(C1H, C1H)
    a2, b2 = pl.ds(C1, C2H), pl.ds(C1 + C2H, C2H)

    project(0, C1H)
    e = {}
    e["p1"] = send(pb.at[far, :, :, a1], rx1.at[0], esend.at[0], erecv.at[0], to_up)
    e["m2"] = send(pb.at[down, :, :, a1], rx1.at[1], esend.at[1], erecv.at[1], to_down)
    project(C1, D)
    e["y2"] = send(pb.at[:, 1 - y, :, pl.ds(C1, C2)], ry2, esend.at[2], erecv.at[2], to_pair)
    project(C1H, C1)
    e["m1"] = send(pb.at[far, :, :, b1], rx1.at[2], esend.at[3], erecv.at[3], to_down)
    e["p2"] = send(pb.at[up, :, :, b1], rx1.at[3], esend.at[4], erecv.at[4], to_up)

    e["p1"].wait_recv()
    ac1[0] = (rx1[0].astype(F32) + pb[up, :, :, 0:C1H].astype(F32)).astype(BF)
    e["p3"] = send(ac1.at[0], rx1.at[4], esend.at[5], erecv.at[5], to_up)
    e["m1"].wait_recv()
    ac1[1] = (rx1[2].astype(F32) + pb[down, :, :, C1H:C1].astype(F32)).astype(BF)
    e["m3"] = send(ac1.at[1], rx1.at[5], esend.at[6], erecv.at[6], to_down)

    e["y2"].wait_recv()
    for i in range(4):
        sx2[i] = (ry2[i].astype(F32) + pb[i, y, :, C1:D].astype(F32)).astype(BF)
    a2, b2 = pl.ds(0, C2H), pl.ds(C2H, C2H)
    e["P1"] = send(sx2.at[far, :, a2], rx2.at[0], esend.at[7], erecv.at[7], to_up)
    e["M1"] = send(sx2.at[far, :, b2], rx2.at[2], esend.at[8], erecv.at[8], to_down)
    e["M2"] = send(sx2.at[down, :, a2], rx2.at[1], esend.at[9], erecv.at[9], to_down)
    e["P2"] = send(sx2.at[up, :, b2], rx2.at[3], esend.at[10], erecv.at[10], to_up)

    def five(own, one, two):
        return own.astype(F32) + one.astype(F32) + two.astype(F32)

    for name in ("m2", "p2", "p3", "m3"):
        e[name].wait_recv()
    sy1[:, 0:C1H] = five(pb[x, 1 - y, :, 0:C1H], rx1[4, 1 - y], rx1[1, 1 - y]).astype(BF)
    sy1[:, C1H:C1] = five(pb[x, 1 - y, :, C1H:C1], rx1[5, 1 - y], rx1[3, 1 - y]).astype(BF)
    e["y1"] = send(sy1, ry1, esend.at[11], erecv.at[11], to_pair)

    e["P1"].wait_recv()
    ac2[0] = (rx2[0].astype(F32) + sx2[up, :, 0:C2H].astype(F32)).astype(BF)
    e["P3"] = send(ac2.at[0], rx2.at[4], esend.at[12], erecv.at[12], to_up)
    e["M1"].wait_recv()
    ac2[1] = (rx2[2].astype(F32) + sx2[down, :, C2H:C2].astype(F32)).astype(BF)
    e["M3"] = send(ac2.at[1], rx2.at[5], esend.at[13], erecv.at[13], to_down)

    e["y1"].wait_recv()
    own_a = five(pb[x, y, :, 0:C1H], rx1[4, y], rx1[1, y])
    out[:, 0:C1H] = (own_a + ry1[:, 0:C1H].astype(F32)).astype(BF)
    own_b = five(pb[x, y, :, C1H:C1], rx1[5, y], rx1[3, y])
    out[:, C1H:C1] = (own_b + ry1[:, C1H:C1].astype(F32)).astype(BF)
    for name in ("M2", "P2", "P3", "M3"):
        e[name].wait_recv()
    out[:, C1:C1 + C2H] = five(sx2[x, :, 0:C2H], rx2[4], rx2[1]).astype(BF)
    out[:, C1 + C2H:D] = five(sx2[x, :, C2H:C2], rx2[5], rx2[3]).astype(BF)

    for copy in pending:
        copy.wait_send()


def local(fresh, rows_index, counts, key_cache, value_cache, q_gain, k_gain, out_weight):
    any_spec = pl.BlockSpec(memory_space=pl.ANY)
    vmem = pl.BlockSpec(memory_space=pltpu.VMEM)
    dma = pltpu.SemaphoreType.DMA
    V = pltpu.VMEM
    return pl.pallas_call(
        kernel,
        out_shape=jax.ShapeDtypeStruct((ROWS, D), BF),
        in_specs=[any_spec, vmem, pl.BlockSpec(memory_space=pltpu.SMEM)] + [any_spec] * 5,
        out_specs=vmem,
        scratch_shapes=[
            V((3, ROWS, D), BF), V((1, D), BF), V((1, D), BF),
            V((L_BLK, GROUP), BF), V((L_BLK, GROUP), BF), V((GROUP, D), BF),
            V((3, NG, ROWS, GROUP), BF), V((3, CAP, GROUP), BF),
            V((SPAN, GROUP), BF), V((384, GROUP), BF),
            V((2, L_BLK, GROUP), BF), V((2, GROUP, L_BLK), BF), V((8, CH, GROUP), BF),
            V((8, GROUP, CH), F32), V((8, 2, 16, CH), F32),
            V((2, 4, GROUP, CH), BF), V((2, 4, 2, 16, CH), F32),
            V((2, 4, GROUP, CH), BF), V((2, 4, 2, 16, CH), F32),
            V((CH, GROUP), BF), V((SPAN, GROUP), BF), V((CAP, GROUP), BF),
            V((4, 2, ROWS, D), BF),
            V((6, 2, ROWS, C1H), BF), V((2, 2, ROWS, C1H), BF),
            V((ROWS, C1), BF), V((ROWS, C1), BF),
            V((4, ROWS, C2), BF), V((4, ROWS, C2), BF),
            V((6, ROWS, C2H), BF), V((2, ROWS, C2H), BF),
            dma((8,)), dma((3, 7)), dma((3, 7)), dma((4,)), dma((4,)), dma((2,)), dma((2,)),
            dma((2, 4, 2)), dma((2, 4, 2)),
            dma((2, 4, 2)), dma((2, 4, 2)), dma((2, 4, 2)), dma((2, 4, 2)),
            dma((4,)), dma((4,)), dma((14,)), dma((14,)),
        ],
        compiler_params=pltpu.CompilerParams(
            collective_id=0, has_side_effects=True, vmem_limit_bytes=56 * 1024 * 1024
        ),
    )(
        jnp.transpose(fresh, (1, 0, 2)), rows_index.reshape(1, CAP), counts, key_cache, value_cache,
        q_gain.reshape(1, D), k_gain.reshape(1, D), out_weight,
    )


def solution(mesh):
    placed = (
        P(("cfg", "blk", "head"), None, None),
        P("blk"),
        P(),
        P(("cfg", "blk"), "head"),
        P(("cfg", "blk"), "head"),
        P(),
        P(),
        P("head", None),
    )
    return jax.shard_map(
        local,
        mesh=mesh,
        in_specs=placed,
        out_specs=P(("cfg", "blk", "head"), None),
        check_vma=False,
    )
```

time: 323 us -> 100 us (0.31); the launches traced: 319 us -> 100 us
  waiting for transfers between devices: 190 us -> 0 us
  Pallas kernels: 0 us -> 95.7 us
  matrix products: 62.8 us -> 0 us
  local copies, waits for them, and re-layouts: 38.1 us -> 4.36 us
  between operations: 14 us -> 0.01 us
  other arithmetic: 8.06 us -> 0 us
  starting transfers between devices: 5.84 us -> 0 us
    all_gather x2 -> x0, waiting for transfers between devices: 115 us -> none  [the longest x1 63.3 us: attend(): lax.all_gather(keys, 'blk', axis=0, tiled=True)]
    pallas_call x0 -> x1, Pallas kernels: none -> 95.7 us  [local(): pl.pallas_call(kernel, out_shape=jax.ShapeDtypeStruct((ROWS, D), BF), in_...]
    dot_general x33 -> x0, matrix products: 62.8 us -> none  [the longest x16 30.5 us: absorb(): jnp.einsum('rhn,nhe->rhe', weights.astype(jnp.bfloat16), values, preferre...]
    reduce_scatter x1 -> x0, waiting for transfers between devices: 61.6 us -> none  [local(): lax.psum_scatter(jnp.dot(attention, out_weight, preferred_element_type=jn...]
    all_gather x2 -> x0, local copies, waits for them, and re-layouts: 28.4 us -> none  [the longest x1 14.2 us: attend(): lax.all_gather(keys, 'blk', axis=0, tiled=True)]
    all_to_all x1 -> x0, waiting for transfers between devices: 12.6 us -> none  [local(): lax.all_to_all(packed, 'head', split_axis=2, concat_axis=0, tiled=True)]
    reduce_sum x17 -> x0, other arithmetic: 7.26 us -> none  [the longest x16 7.01 us: absorb(): totals = totals * factor + jnp.sum(weights, axis=-1)]
    scatter x4 -> x0, local copies, waits for them, and re-layouts: 6.16 us -> none  [the longest x2 3.08 us: local(): keys = key_cache.at[targets].set(fresh_k, mode='drop')]
  transfers between devices with their start and end apart: 4 -> 0, of which waited for: 4 -> 0; matrix products, arithmetic and copies ran while one was open for 6% -> 0% of each run, Pallas kernels for 0% -> 0%
where the time goes in v1:
time: 100 us
  Pallas kernels  95.7 us (96%)
  local copies, waits for them, and re-layouts  4.36 us (4%)
    pallas_call x1, Pallas kernels, local(): pl.pallas_call(kernel, out_shape=jax.ShapeDtypeStruct((ROWS, D), BF), in_...  95.7 us

profile of v1, /device:TPU:8, one launch (start us, length us, event | category | flops | bytes accessed | tf_op | source)
XLA Modules:
  0.0 100.1 jit_solution(15870905557997501954)
XLA Ops:
  0.0 1.3 %reshape.10.qgain = bf16[1,5120]{1,0:T(2,128)(2,1)} reshape(bf16[5120]{0:T(1024)(128)(2,1)} %param.13) | data formatting | bytes 20480 | tf_op jit(solution)/shard_map/reshape | solution.py:405
  1.3 1.3 %reshape.11.kgain = bf16[1,5120]{1,0:T(2,128)(2,1)} reshape(bf16[5120]{0:T(1024)(128)(2,1)} %param.14) | data formatting | bytes 20480 | tf_op jit(solution)/shard_map/reshape | solution.py:405
  2.6 95.7 %shard_map.82 = bf16[32,5120]{1,0:T(8,128)(2,1)} custom-call(bf16[3,32,5120]{2,1,0:T(8,128)(2,1)} %bitcast.2, s32[1,256]{1,0:T(1,128)} %bitcast.3, s32[16]{0:T(128)} %counts.1, bf16[512,640]{1,0:T(8,128)(2,1)} %kcache.1, bf16[512,640]{1,0:T(8,128)(2,1)} %vcache.1, bf16[1,5120]{1,0:T(2,128)(2,1)} %reshape.10.qgain, bf16[1,5120]{1,0:T(2,128)(2,1)} %reshape.11.kgain, ...), custom_call_target="tpu_custom_call" | custom-call | tf_op jit(solution)/shard_map/pallas_call | solution.py:375
  98.4 1.7 %copy.10 = bf16[32,5120]{1,0:T(8,128)(2,1)} copy(bf16[32,5120]{1,0:T(8,128)(2,1)} %shard_map.82) | data formatting | bytes 655360

commit v2 on v1

--- a/solution.py
+++ b/solution.py
@@ -44,7 +44,7 @@
 def kernel(
     fresh, ridx, counts, kcache, vcache, qgain, kgain, weight, out,
     fv, gq, gk, kc, vc, wv, sent, got, selq, rbuf, kfull, vt, qs,
-    of, st, so, ss, ro, rs, abuf, cat, att, pb,
+    of, st, so, ss, ro, rs, abuf, cat, back, att, pb,
     rx1, ac1, ry1, sy1, ry2, sx2, rx2, ac2,
     lsem, asend, arecv, rsend, rrecv, ksend, krecv, gsend, grecv,
     dsend, drecv, tsend, trecv, usend, urecv, esend, erecv,
@@ -88,7 +88,6 @@
         pl.semaphore_signal(barrier, inc=1, device_id={"head": head_at(dx, dy)}, device_id_type=MESH)
     for offset in (-2, -1, 1, 2):
         pl.semaphore_signal(barrier, inc=1, device_id=blk_at(offset), device_id_type=MESH)
-    pl.semaphore_wait(barrier, len(pairs) + 4)
 
     live = counts[j]
     before = jnp.int32(0)
@@ -98,37 +97,56 @@
 
     my_rows = pl.ds(pl.multiple_of(h * ROWS, ROWS), ROWS)
     a_copies = [[], [], []]
-    for t in range(3):
+
+    def prepare(t):
         loads[2 * t].wait()
-        if t < 2:
+        if t == 2:
+            for g in range(NG):
+                sent[t, g] = fv[t, :, g * GROUP:(g + 1) * GROUP]
+        else:
             loads[2 * t + 1].wait()
             rows = fv[t].astype(F32)
-            mean_sq = jnp.mean(rows * rows, axis=-1, keepdims=True)
+            factor = lax.rsqrt(jnp.mean(rows * rows, axis=-1, keepdims=True) + EPS)
             gains = (gq if t == 0 else gk)[...].astype(F32)
-            rows = (rows * lax.rsqrt(mean_sq + EPS) * gains).astype(BF)
-        else:
-            rows = fv[2]
-        for g in range(NG):
-            sent[t, g] = rows[:, g * GROUP:(g + 1) * GROUP]
+            for c in range(D // HEAD_DIM):
+                cols = slice(c * HEAD_DIM, (c + 1) * HEAD_DIM)
+                to = slice(c % NH * HEAD_DIM, (c % NH + 1) * HEAD_DIM)
+                sent[t, c // NH, :, to] = (rows[:, cols] * factor * gains[c:c + 1]).astype(BF)
+        got[t, my_rows] = sent[t, h]
+
+    def spread(t):
         for n, (dx, dy) in enumerate(pairs):
             peer = head_at(dx, dy)
             a_copies[t].append(send(
                 sent.at[t, peer], got.at[t, my_rows], asend.at[t, n], arecv.at[t, n], {"head": peer}
             ))
-        got[t, my_rows] = sent[t, h]
-
+
+    prepare(0)
+    pl.semaphore_wait(barrier, len(pairs) + 4)
+    spread(0)
+    prepare(1)
+    prepare(2)
+
+    r_id = lax.broadcasted_iota(jnp.int32, (SPAN, CAP), 0)
+    s_id = lax.broadcasted_iota(jnp.int32, (1, CAP), 1)
+    place = jnp.where(r_id == jnp.where(s_id < live, s_id + shift, -1), 1.0, 0.0).astype(BF)
     for copy in a_copies[0]:
         copy.wait_recv()
-    r_id = lax.broadcasted_iota(jnp.int32, (SPAN, CAP), 0)
-    s_id = lax.broadcasted_iota(jnp.int32, (SPAN, CAP), 1)
-    place = ((r_id - s_id) == shift) & (s_id < live)
-    selq[...] = mm(place.astype(F32).astype(BF), got[0]).astype(BF)
+    selq[...] = mm(place, got[0]).astype(BF)
     r_copies = [
         send(selq.at[pl.ds(first, size)], rbuf.at[pl.ds(to, size)], rsend.at[n], rrecv.at[n], blk_at(offset))
         for n, (first, size, to, offset) in enumerate(
             ((64, 128, 0, -1), (320, 128, 128, 1), (0, 64, 256, -2), (448, 64, 320, 2))
         )
     ]
+    spread(1)
+    spread(2)
+    back[...] = place.T
+    st[...] = jnp.zeros_like(st)
+    pos = lax.broadcasted_iota(jnp.int32, (L_BLK, CAP), 0)
+    hits = jnp.where(pos == jnp.where(s_id < live, ridx[...], -1), 1.0, 0.0)
+    hit = jnp.sum(hits, axis=1, keepdims=True) > 0.5
+    hits = hits.astype(BF)
     for copy in r_copies:
         copy.wait_recv()
     mine = (selq[192:320].astype(F32) + rbuf[0:128].astype(F32)) + rbuf[128:256].astype(F32)
@@ -153,17 +171,15 @@
         return copies
 
     g_copies = gather_step(1)
+    for copy in g_copies:
+        copy.wait_recv()
+    g_copies = gather_step(2)
 
     for t in (1, 2):
         for copy in a_copies[t]:
             copy.wait_recv()
     loads[5].wait()
     loads[6].wait()
-    pos = lax.broadcasted_iota(jnp.int32, (L_BLK, CAP), 0)
-    slot = lax.broadcasted_iota(jnp.int32, (L_BLK, CAP), 1)
-    hits = ((pos == ridx[...]) & (slot < live)).astype(F32)
-    hit = jnp.sum(hits, axis=1, keepdims=True) > 0.5
-    hits = hits.astype(BF)
     kfull[0] = jnp.where(hit, mm(hits, got[1]), kc[...].astype(F32)).astype(BF)
     k_copy = send(kfull.at[0], kfull.at[1], ksend.at[0], krecv.at[0], sibling)
     vt[0] = jnp.where(hit, mm(hits, got[2]), vc[...].astype(F32)).T.astype(BF)
@@ -191,16 +207,12 @@
                 st[s, part, row:row + 1, :] = top[:, lanes]
                 st[s, part, 8 + row:9 + row, :] = total[:, lanes]
 
-    st[...] = jnp.zeros_like(st)
     for copy in g_copies:
         copy.wait_recv()
-    g_copies = gather_step(2)
+    g_copies = gather_step(3)
     k_copy.wait_recv()
     v_copy.wait_recv()
     attend((7, 1))
-    for copy in g_copies:
-        copy.wait_recv()
-    g_copies = gather_step(3)
     attend((6, 2))
     for copy in g_copies:
         copy.wait_recv()
@@ -288,19 +300,16 @@
         )
     ]
     cat[192:320] = abuf[...]
-    r_id = lax.broadcasted_iota(jnp.int32, (CAP, SPAN), 1)
-    s_id = lax.broadcasted_iota(jnp.int32, (CAP, SPAN), 0)
-    place = (((r_id - s_id) == shift) & (s_id < live)).astype(F32).astype(BF)
     for copy in u_copies:
         copy.wait_recv()
-    att[...] = mm(place, cat[...]).astype(BF)
+    att[...] = mm(back[...], cat[...]).astype(BF)
 
     loads[7].wait()
 
     def project(first, last):
-        @pl.loop(first // 256, last // 256)
+        @pl.loop(first // 512, last // 512)
         def _(i):
-            cols = pl.ds(pl.multiple_of(i * 256, 256), 256)
+            cols = pl.ds(pl.multiple_of(i * 512, 512), 512)
             tile = mm(att[...], wv[:, cols]).astype(BF)
             for g in range(NG):
                 pb[g // 2, g % 2, :, cols] = tile[g * ROWS:(g + 1) * ROWS]
@@ -315,11 +324,13 @@
     e = {}
     e["p1"] = send(pb.at[far, :, :, a1], rx1.at[0], esend.at[0], erecv.at[0], to_up)
     e["m2"] = send(pb.at[down, :, :, a1], rx1.at[1], esend.at[1], erecv.at[1], to_down)
-    project(C1, D)
-    e["y2"] = send(pb.at[:, 1 - y, :, pl.ds(C1, C2)], ry2, esend.at[2], erecv.at[2], to_pair)
+    project(C1, C1 + C2H)
+    e["y2"] = send(pb.at[:, 1 - y, :, a2], ry2.at[:, :, 0:C2H], esend.at[2], erecv.at[2], to_pair)
     project(C1H, C1)
     e["m1"] = send(pb.at[far, :, :, b1], rx1.at[2], esend.at[3], erecv.at[3], to_down)
     e["p2"] = send(pb.at[up, :, :, b1], rx1.at[3], esend.at[4], erecv.at[4], to_up)
+    project(C1 + C2H, D)
+    e["y3"] = send(pb.at[:, 1 - y, :, b2], ry2.at[:, :, C2H:C2], esend.at[14], erecv.at[14], to_pair)
 
     e["p1"].wait_recv()
     ac1[0] = (rx1[0].astype(F32) + pb[up, :, :, 0:C1H].astype(F32)).astype(BF)
@@ -329,6 +340,7 @@
     e["m3"] = send(ac1.at[1], rx1.at[5], esend.at[6], erecv.at[6], to_down)
 
     e["y2"].wait_recv()
+    e["y3"].wait_recv()
     for i in range(4):
         sx2[i] = (ry2[i].astype(F32) + pb[i, y, :, C1:D].astype(F32)).astype(BF)
     a2, b2 = pl.ds(0, C2H), pl.ds(C2H, C2H)
@@ -378,7 +390,7 @@
         in_specs=[any_spec, vmem, pl.BlockSpec(memory_space=pltpu.SMEM)] + [any_spec] * 5,
         out_specs=vmem,
         scratch_shapes=[
-            V((3, ROWS, D), BF), V((1, D), BF), V((1, D), BF),
+            V((3, ROWS, D), BF), V((D // 128, 128), BF), V((D // 128, 128), BF),
             V((L_BLK, GROUP), BF), V((L_BLK, GROUP), BF), V((GROUP, D), BF),
             V((3, NG, ROWS, GROUP), BF), V((3, CAP, GROUP), BF),
             V((SPAN, GROUP), BF), V((384, GROUP), BF),
@@ -386,7 +398,7 @@
             V((8, GROUP, CH), F32), V((8, 2, 16, CH), F32),
             V((2, 4, GROUP, CH), BF), V((2, 4, 2, 16, CH), F32),
             V((2, 4, GROUP, CH), BF), V((2, 4, 2, 16, CH), F32),
-            V((CH, GROUP), BF), V((SPAN, GROUP), BF), V((CAP, GROUP), BF),
+            V((CH, GROUP), BF), V((SPAN, GROUP), BF), V((CAP, SPAN), BF), V((CAP, GROUP), BF),
             V((4, 2, ROWS, D), BF),
             V((6, 2, ROWS, C1H), BF), V((2, 2, ROWS, C1H), BF),
             V((ROWS, C1), BF), V((ROWS, C1), BF),
@@ -395,14 +407,14 @@
             dma((8,)), dma((3, 7)), dma((3, 7)), dma((4,)), dma((4,)), dma((2,)), dma((2,)),
             dma((2, 4, 2)), dma((2, 4, 2)),
             dma((2, 4, 2)), dma((2, 4, 2)), dma((2, 4, 2)), dma((2, 4, 2)),
-            dma((4,)), dma((4,)), dma((14,)), dma((14,)),
+            dma((4,)), dma((4,)), dma((15,)), dma((15,)),
         ],
         compiler_params=pltpu.CompilerParams(
             collective_id=0, has_side_effects=True, vmem_limit_bytes=56 * 1024 * 1024
         ),
     )(
         jnp.transpose(fresh, (1, 0, 2)), rows_index.reshape(1, CAP), counts, key_cache, value_cache,
-        q_gain.reshape(1, D), k_gain.reshape(1, D), out_weight,
+        q_gain.reshape(D // 128, 128), k_gain.reshape(D // 128, 128), out_weight,
     )
 
 

time: 100 us -> 96.3 us (0.963); the launches traced: 100 us -> 94.4 us
  Pallas kernels: 95.7 us -> 92.7 us
  local copies, waits for them, and re-layouts: 4.36 us -> 1.72 us
    pallas_call x1, Pallas kernels: 95.7 us -> 92.7 us  [local(): pl.pallas_call(kernel, out_shape=jax.ShapeDtypeStruct((ROWS, D), BF), in_...]
    reshape x2 -> x0, local copies, waits for them, and re-layouts: 2.64 us -> none  [the longest x1 1.32 us: local(): k_gain.reshape(1, D)]
where the time goes in v2:
time: 96.3 us; the launch traced here: 94.4 us
  Pallas kernels  92.7 us (96%)
  local copies, waits for them, and re-layouts  1.72 us (2%)
    pallas_call x1, Pallas kernels, local(): pl.pallas_call(kernel, out_shape=jax.ShapeDtypeStruct((ROWS, D), BF), in_...  92.7 us

profile of v2, /device:TPU:8, one launch (start us, length us, event | category | flops | bytes accessed | tf_op | source)
XLA Modules:
  0.0 94.4 jit_solution(1676380891382404273)
XLA Ops:
  0.0 92.7 %shard_map.82 = bf16[32,5120]{1,0:T(8,128)(2,1)} custom-call(bf16[3,32,5120]{2,1,0:T(8,128)(2,1)} %bitcast.4, s32[1,256]{1,0:T(1,128)} %bitcast.7, s32[16]{0:T(128)} %counts.1, bf16[512,640]{1,0:T(8,128)(2,1)} %kcache.1, bf16[512,640]{1,0:T(8,128)(2,1)} %vcache.1, bf16[40,128]{1,0:T(8,128)(2,1)} %bitcast.5, bf16[40,128]{1,0:T(8,128)(2,1)} %bitcast.6, ...), custom_call_target="tpu_custom_call" | custom-call | tf_op jit(solution)/shard_map/pallas_call | solution.py:387
  92.7 1.7 %copy.10 = bf16[32,5120]{1,0:T(8,128)(2,1)} copy(bf16[32,5120]{1,0:T(8,128)(2,1)} %shard_map.82) | data formatting | bytes 655360

commit v3 on v2

--- a/solution.py
+++ b/solution.py
@@ -25,7 +25,10 @@
 CH = 128
 SPAN = 512
 BASE = 192
-PART = ((0, 3), (3, 5))
+PIECES = ((0, 2), (2, 4), (4, 5))
+NP = len(PIECES)
+WIDTH = tuple((last - first) * HEAD_DIM for first, last in PIECES)
+LONG = ((0,), (1, 2))
 C1 = 3072
 C1H = C1 // 2
 C2 = D - C1
@@ -43,10 +46,10 @@
 
 def kernel(
     fresh, ridx, counts, kcache, vcache, qgain, kgain, weight, out,
-    fv, gq, gk, kc, vc, wv, sent, got, selq, rbuf, kfull, vt, qs,
+    fv, gq, gk, kc, vc, wv, sent, got, sentq, gotq, selq, rbuf, kfull, vt, qs,
     of, st, so, ss, ro, rs, abuf, cat, back, att, pb,
     rx1, ac1, ry1, sy1, ry2, sx2, rx2, ac2,
-    lsem, asend, arecv, rsend, rrecv, ksend, krecv, gsend, grecv,
+    lsem, qsend, qrecv, asend, arecv, rsend, rrecv, ksend, krecv, gsend, grecv,
     dsend, drecv, tsend, trecv, usend, urecv, esend, erecv,
 ):
     j = lax.axis_index("blk")
@@ -79,7 +82,7 @@
             (fresh.at[2], fv.at[2]), (kcache, kc), (vcache, vc), (weight, wv),
         ))
     ]
-    for load in loads:
+    for load in loads[:6]:
         load.start()
 
     barrier = pltpu.get_barrier_semaphore()
@@ -96,23 +99,39 @@
     shift = before - CH * j + BASE
 
     my_rows = pl.ds(pl.multiple_of(h * ROWS, ROWS), ROWS)
-    a_copies = [[], [], []]
+    a_copies = [[], []]
+    q_copies = [[] for _ in PIECES]
+
+    def piece_of(head):
+        for p, (first, last) in enumerate(PIECES):
+            if head < last:
+                return p, head - first
 
     def prepare(t):
         loads[2 * t].wait()
         if t == 2:
             for g in range(NG):
-                sent[t, g] = fv[t, :, g * GROUP:(g + 1) * GROUP]
+                sent[1, g] = fv[t, :, g * GROUP:(g + 1) * GROUP]
+            got[1, my_rows] = sent[1, h]
+            return
+        loads[2 * t + 1].wait()
+        rows = fv[t].astype(F32)
+        factor = lax.rsqrt(jnp.mean(rows * rows, axis=-1, keepdims=True) + EPS)
+        gains = (gq if t == 0 else gk)[...].astype(F32)
+        for c in range(D // HEAD_DIM):
+            cols = slice(c * HEAD_DIM, (c + 1) * HEAD_DIM)
+            g, i = c // NH, c % NH
+            value = (rows[:, cols] * factor * gains[c:c + 1]).astype(BF)
+            if t == 0:
+                p, n = piece_of(i)
+                sentq[p][g, :, n * HEAD_DIM:(n + 1) * HEAD_DIM] = value
+            else:
+                sent[0, g, :, i * HEAD_DIM:(i + 1) * HEAD_DIM] = value
+        if t == 0:
+            for p in range(NP):
+                gotq[p][my_rows] = sentq[p][h]
         else:
-            loads[2 * t + 1].wait()
-            rows = fv[t].astype(F32)
-            factor = lax.rsqrt(jnp.mean(rows * rows, axis=-1, keepdims=True) + EPS)
-            gains = (gq if t == 0 else gk)[...].astype(F32)
-            for c in range(D // HEAD_DIM):
-                cols = slice(c * HEAD_DIM, (c + 1) * HEAD_DIM)
-                to = slice(c % NH * HEAD_DIM, (c % NH + 1) * HEAD_DIM)
-                sent[t, c // NH, :, to] = (rows[:, cols] * factor * gains[c:c + 1]).astype(BF)
-        got[t, my_rows] = sent[t, h]
+            got[0, my_rows] = sent[0, h]
 
     def spread(t):
         for n, (dx, dy) in enumerate(pairs):
@@ -123,76 +142,84 @@
 
     prepare(0)
     pl.semaphore_wait(barrier, len(pairs) + 4)
-    spread(0)
+    for p in range(NP):
+        for n, (dx, dy) in enumerate(pairs):
+            peer = head_at(dx, dy)
+            q_copies[p].append(send(
+                sentq[p].at[peer], gotq[p].at[my_rows], qsend.at[p, n], qrecv.at[p, n], {"head": peer}
+            ))
+    for load in loads[6:]:
+        load.start()
     prepare(1)
     prepare(2)
 
     r_id = lax.broadcasted_iota(jnp.int32, (SPAN, CAP), 0)
     s_id = lax.broadcasted_iota(jnp.int32, (1, CAP), 1)
     place = jnp.where(r_id == jnp.where(s_id < live, s_id + shift, -1), 1.0, 0.0).astype(BF)
-    for copy in a_copies[0]:
-        copy.wait_recv()
-    selq[...] = mm(place, got[0]).astype(BF)
-    r_copies = [
-        send(selq.at[pl.ds(first, size)], rbuf.at[pl.ds(to, size)], rsend.at[n], rrecv.at[n], blk_at(offset))
-        for n, (first, size, to, offset) in enumerate(
-            ((64, 128, 0, -1), (320, 128, 128, 1), (0, 64, 256, -2), (448, 64, 320, 2))
-        )
-    ]
-    spread(1)
-    spread(2)
+    r_copies = []
+    for p in range(NP):
+        for copy in q_copies[p]:
+            copy.wait_recv()
+        selq[p][...] = mm(place, gotq[p][...]).astype(BF)
+        r_copies.append([
+            send(selq[p].at[pl.ds(first, size)], rbuf[p].at[pl.ds(to, size)],
+                 rsend.at[p, n], rrecv.at[p, n], blk_at(offset))
+            for n, (first, size, to, offset) in enumerate(
+                ((64, 128, 0, -1), (320, 128, 128, 1), (0, 64, 256, -2), (448, 64, 320, 2))
+            )
+        ])
+        if p < 2:
+            spread(p)
     back[...] = place.T
     st[...] = jnp.zeros_like(st)
     pos = lax.broadcasted_iota(jnp.int32, (L_BLK, CAP), 0)
     hits = jnp.where(pos == jnp.where(s_id < live, ridx[...], -1), 1.0, 0.0)
     hit = jnp.sum(hits, axis=1, keepdims=True) > 0.5
     hits = hits.astype(BF)
-    for copy in r_copies:
-        copy.wait_recv()
-    mine = (selq[192:320].astype(F32) + rbuf[0:128].astype(F32)) + rbuf[128:256].astype(F32)
-    qs[0, 0:64] = (mine[0:64] + rbuf[320:384].astype(F32)).astype(BF)
-    qs[0, 64:128] = (mine[64:128] + rbuf[256:320].astype(F32)).astype(BF)
-
-    halves = (pl.ds(0, 64), pl.ds(64, 64))
+
+    g_copies = {}
+
+    def gather_send(way, step, p):
+        src = (8 - (step - 1)) % 8 if way == 0 else step - 1
+        dst = 8 - step if way == 0 else step
+        g_copies[way, step, p] = send(
+            qs[p].at[src], qs[p].at[dst],
+            gsend.at[way, step - 1, p], grecv.at[way, step - 1, p], blk_at(2 if way == 0 else -2),
+        )
 
     def gather_step(step):
-        copies = []
-        for half in range(2):
+        for p in range(NP):
             for way in range(2):
-                if step == 4 and half != way:
-                    continue
-                src = (8 - (step - 1)) % 8 if way == 0 else step - 1
-                dst = 8 - step if way == 0 else step
-                copies.append(send(
-                    qs.at[src, halves[half]], qs.at[dst, halves[half]],
-                    gsend.at[way, step - 1, half], grecv.at[way, step - 1, half],
-                    blk_at(2 if way == 0 else -2),
-                ))
-        return copies
-
-    g_copies = gather_step(1)
-    for copy in g_copies:
-        copy.wait_recv()
-    g_copies = gather_step(2)
-
-    for t in (1, 2):
+                g_copies[way, step - 1, p].wait_recv()
+                if step < 4 or p in LONG[way]:
+                    gather_send(way, step, p)
+
+    for p in range(NP):
+        for copy in r_copies[p]:
+            copy.wait_recv()
+        mine = (selq[p][192:320].astype(F32) + rbuf[p][0:128].astype(F32)) + rbuf[p][128:256].astype(F32)
+        qs[p][0, 0:64] = (mine[0:64] + rbuf[p][320:384].astype(F32)).astype(BF)
+        qs[p][0, 64:128] = (mine[64:128] + rbuf[p][256:320].astype(F32)).astype(BF)
+        gather_send(0, 1, p)
+        gather_send(1, 1, p)
+    gather_step(2)
+
+    for t in range(2):
         for copy in a_copies[t]:
             copy.wait_recv()
     loads[5].wait()
     loads[6].wait()
-    kfull[0] = jnp.where(hit, mm(hits, got[1]), kc[...].astype(F32)).astype(BF)
+    kfull[0] = jnp.where(hit, mm(hits, got[0]), kc[...].astype(F32)).astype(BF)
     k_copy = send(kfull.at[0], kfull.at[1], ksend.at[0], krecv.at[0], sibling)
-    vt[0] = jnp.where(hit, mm(hits, got[2]), vc[...].astype(F32)).T.astype(BF)
+    vt[0] = jnp.where(hit, mm(hits, got[1]), vc[...].astype(F32)).T.astype(BF)
     v_copy = send(vt.at[0], vt.at[1], ksend.at[1], krecv.at[1], sibling)
 
-    def attend(slots):
-        width = CH * len(slots)
-        for i in range(NH):
+    def attend(slots, heads):
+        for i in heads:
+            p, k = piece_of(i)
             cols = slice(i * HEAD_DIM, (i + 1) * HEAD_DIM)
-            if len(slots) == 1:
-                query = qs[slots[0], :, cols]
-            else:
-                query = jnp.concatenate([qs[s, :, cols] for s in slots], axis=0)
+            query = [qs[p][s, :, k * HEAD_DIM:(k + 1) * HEAD_DIM] for s in slots]
+            query = query[0] if len(slots) == 1 else jnp.concatenate(query, axis=0)
             s0 = nt(kfull[0, :, cols], query)
             s1 = nt(kfull[1, :, cols], query)
             top = jnp.maximum(jnp.max(s0, axis=0, keepdims=True), jnp.max(s1, axis=0, keepdims=True)) * SCALE2
@@ -200,36 +227,24 @@
             p1 = jnp.exp2(s1 * SCALE2 - top)
             total = jnp.sum(p0, axis=0, keepdims=True) + jnp.sum(p1, axis=0, keepdims=True)
             o = mm(vt[0, cols, :], p0.astype(BF)) + mm(vt[1, cols, :], p1.astype(BF))
-            part, row = (0, i) if i < 3 else (1, i - 3)
             for n, s in enumerate(slots):
                 lanes = slice(n * CH, (n + 1) * CH)
                 of[s, cols, :] = o[:, lanes]
-                st[s, part, row:row + 1, :] = top[:, lanes]
-                st[s, part, 8 + row:9 + row, :] = total[:, lanes]
-
-    for copy in g_copies:
-        copy.wait_recv()
-    g_copies = gather_step(3)
+                st[s, p, k:k + 1, :] = top[:, lanes]
+                st[s, p, 4 + k:5 + k, :] = total[:, lanes]
+
+    gather_step(3)
     k_copy.wait_recv()
     v_copy.wait_recv()
-    attend((7, 1))
-    attend((6, 2))
-    for copy in g_copies:
-        copy.wait_recv()
-    g_copies = gather_step(4)
-    attend((5, 3))
-    for copy in g_copies:
-        copy.wait_recv()
-    attend((4,))
-
-    def part_rows(part):
-        first, last = PART[part]
-        return pl.ds(first * HEAD_DIM, (last - first) * HEAD_DIM)
-
-    def joined(slot, part, arrivals):
-        first, last = PART[part]
-        tops = [st[slot, part, 0:8]] + [rs[way, step, part, 0:8] for way, step in arrivals]
-        sums = [st[slot, part, 8:16]] + [rs[way, step, part, 8:16] for way, step in arrivals]
+    attend((7, 1), range(3))
+    gather_step(4)
+    attend((7, 1), range(3, NH))
+    attend((6, 2), range(NH))
+
+    def joined(slot, p, arrivals):
+        first, last = PIECES[p]
+        tops = [st[slot, p, 0:4]] + [rs[way, step, p, 0:4] for way, step in arrivals]
+        sums = [st[slot, p, 4:8]] + [rs[way, step, p, 4:8] for way, step in arrivals]
         top = functools.reduce(jnp.maximum, tops)
         factors = [jnp.exp2(t - top) for t in tops]
         total = sum(a * f for a, f in zip(sums, factors))
@@ -245,64 +260,71 @@
 
     d_copies = {}
 
-    def give(way, step, part):
+    def give(way, step, p):
         ahead = 5 - step
         slot = ahead if way == 0 else 8 - ahead
-        first_step = 1 if part == way else 2
-        if step > first_step:
-            for copy in d_copies[way, step - 1, part]:
+        first, last = PIECES[p]
+        if step > (1 if p in LONG[way] else 2):
+            for copy in d_copies[way, step - 1, p]:
                 copy.wait_recv()
-            values, top, total = joined(slot, part, [(way, step - 2)])
+            values, top, total = joined(slot, p, [(way, step - 2)])
         else:
-            first, last = PART[part]
             values = [of[slot, i * HEAD_DIM:(i + 1) * HEAD_DIM, :] for i in range(first, last)]
-            top, total = st[slot, part, 0:8], st[slot, part, 8:16]
+            top, total = st[slot, p, 0:4], st[slot, p, 4:8]
         for n, value in enumerate(values):
-            i = PART[part][0] + n
+            i = first + n
             so[way, step - 1, i * HEAD_DIM:(i + 1) * HEAD_DIM, :] = value.astype(BF)
-        ss[way, step - 1, part, 0:8] = top
-        ss[way, step - 1, part, 8:16] = total
-        rows = part_rows(part)
+        ss[way, step - 1, p, 0:4] = top
+        ss[way, step - 1, p, 4:8] = total
+        rows = pl.ds(first * HEAD_DIM, WIDTH[p])
         dev = blk_at(2 if way == 0 else -2)
-        d_copies[way, step, part] = [
-            send(ss.at[way, step - 1, part], rs.at[way, step - 1, part],
-                 tsend.at[way, step - 1, part], trecv.at[way, step - 1, part], dev),
+        d_copies[way, step, p] = [
+            send(ss.at[way, step - 1, p], rs.at[way, step - 1, p],
+                 tsend.at[way, step - 1, p], trecv.at[way, step - 1, p], dev),
             send(so.at[way, step - 1, rows], ro.at[way, step - 1, rows],
-                 dsend.at[way, step - 1, part], drecv.at[way, step - 1, part], dev),
+                 dsend.at[way, step - 1, p], drecv.at[way, step - 1, p], dev),
         ]
 
-    give(0, 1, 0)
-    give(1, 1, 1)
-    give(0, 2, 1)
-    give(1, 2, 0)
-    attend((0,))
-    give(0, 2, 0)
-    give(1, 2, 1)
+    for p in range(NP):
+        way = 0 if p in LONG[0] else 1
+        g_copies[way, 4, p].wait_recv()
+        attend((4,), range(*PIECES[p]))
+        give(way, 1, p)
+    for way in range(2):
+        for p in LONG[1 - way]:
+            attend((5, 3), range(*PIECES[p]))
+            give(way, 2, p)
+    for way in range(2):
+        for p in LONG[way]:
+            give(way, 2, p)
+    attend((0,), range(NH))
+    order = ((0, 1), (1, 0), (0, 2), (0, 0), (1, 1), (1, 2))
     for step in (3, 4):
-        give(0, step, 1)
-        give(1, step, 0)
-        give(0, step, 0)
-        give(1, step, 1)
-    for part in (1, 0):
+        for way, p in order:
+            give(way, step, p)
+
+    u_copies = {}
+    for p in (1, 0, 2):
         for way in range(2):
-            for copy in d_copies[way, 4, part]:
+            for copy in d_copies[way, 4, p]:
                 copy.wait_recv()
-        values, _, total = joined(0, part, [(0, 3), (1, 3)])
+        values, _, total = joined(0, p, [(0, 3), (1, 3)])
         for n, value in enumerate(values):
-            i = PART[part][0] + n
             result = (value / total[n:n + 1]).T.astype(BF)
-            abuf[:, i * HEAD_DIM:(i + 1) * HEAD_DIM] = result
-
-    u_copies = [
-        send(abuf.at[pl.ds(first, size)], cat.at[pl.ds(to, size)], usend.at[n], urecv.at[n], blk_at(offset))
-        for n, (first, size, to, offset) in enumerate(
-            ((0, 128, 320, -1), (0, 128, 64, 1), (0, 64, 448, -2), (64, 64, 0, 2))
-        )
-    ]
-    cat[192:320] = abuf[...]
-    for copy in u_copies:
-        copy.wait_recv()
-    att[...] = mm(back[...], cat[...]).astype(BF)
+            abuf[p][:, n * HEAD_DIM:(n + 1) * HEAD_DIM] = result
+        u_copies[p] = [
+            send(abuf[p].at[pl.ds(first, size)], cat[p].at[pl.ds(to, size)],
+                 usend.at[p, n], urecv.at[p, n], blk_at(offset))
+            for n, (first, size, to, offset) in enumerate(
+                ((0, 128, 320, -1), (0, 128, 64, 1), (0, 64, 448, -2), (64, 64, 0, 2))
+            )
+        ]
+        cat[p][192:320] = abuf[p][...]
+    for p in (1, 0, 2):
+        for copy in u_copies[p]:
+            copy.wait_recv()
+        first = PIECES[p][0] * HEAD_DIM
+        att[:, first:first + WIDTH[p]] = mm(back[...], cat[p][...]).astype(BF)
 
     loads[7].wait()
 
@@ -384,6 +406,10 @@
     vmem = pl.BlockSpec(memory_space=pltpu.VMEM)
     dma = pltpu.SemaphoreType.DMA
     V = pltpu.VMEM
+
+    def by_piece(*dims):
+        return [V(dims + (width,), BF) for width in WIDTH]
+
     return pl.pallas_call(
         kernel,
         out_shape=jax.ShapeDtypeStruct((ROWS, D), BF),
@@ -392,22 +418,23 @@
         scratch_shapes=[
             V((3, ROWS, D), BF), V((D // 128, 128), BF), V((D // 128, 128), BF),
             V((L_BLK, GROUP), BF), V((L_BLK, GROUP), BF), V((GROUP, D), BF),
-            V((3, NG, ROWS, GROUP), BF), V((3, CAP, GROUP), BF),
-            V((SPAN, GROUP), BF), V((384, GROUP), BF),
-            V((2, L_BLK, GROUP), BF), V((2, GROUP, L_BLK), BF), V((8, CH, GROUP), BF),
-            V((8, GROUP, CH), F32), V((8, 2, 16, CH), F32),
-            V((2, 4, GROUP, CH), BF), V((2, 4, 2, 16, CH), F32),
-            V((2, 4, GROUP, CH), BF), V((2, 4, 2, 16, CH), F32),
-            V((CH, GROUP), BF), V((SPAN, GROUP), BF), V((CAP, SPAN), BF), V((CAP, GROUP), BF),
+            V((2, NG, ROWS, GROUP), BF), V((2, CAP, GROUP), BF),
+            by_piece(NG, ROWS), by_piece(CAP), by_piece(SPAN), by_piece(384),
+            V((2, L_BLK, GROUP), BF), V((2, GROUP, L_BLK), BF), by_piece(8, CH),
+            V((8, GROUP, CH), F32), V((8, NP, 8, CH), F32),
+            V((2, 4, GROUP, CH), BF), V((2, 4, NP, 8, CH), F32),
+            V((2, 4, GROUP, CH), BF), V((2, 4, NP, 8, CH), F32),
+            by_piece(CH), by_piece(SPAN), V((CAP, SPAN), BF), V((CAP, GROUP), BF),
             V((4, 2, ROWS, D), BF),
             V((6, 2, ROWS, C1H), BF), V((2, 2, ROWS, C1H), BF),
             V((ROWS, C1), BF), V((ROWS, C1), BF),
             V((4, ROWS, C2), BF), V((4, ROWS, C2), BF),
             V((6, ROWS, C2H), BF), V((2, ROWS, C2H), BF),
-            dma((8,)), dma((3, 7)), dma((3, 7)), dma((4,)), dma((4,)), dma((2,)), dma((2,)),
-            dma((2, 4, 2)), dma((2, 4, 2)),
-            dma((2, 4, 2)), dma((2, 4, 2)), dma((2, 4, 2)), dma((2, 4, 2)),
-            dma((4,)), dma((4,)), dma((15,)), dma((15,)),
+            dma((8,)), dma((NP, 7)), dma((NP, 7)), dma((2, 7)), dma((2, 7)),
+            dma((NP, 4)), dma((NP, 4)), dma((2,)), dma((2,)),
+            dma((2, 4, NP)), dma((2, 4, NP)),
+            dma((2, 4, NP)), dma((2, 4, NP)), dma((2, 4, NP)), dma((2, 4, NP)),
+            dma((NP, 4)), dma((NP, 4)), dma((15,)), dma((15,)),
         ],
         compiler_params=pltpu.CompilerParams(
             collective_id=0, has_side_effects=True, vmem_limit_bytes=56 * 1024 * 1024

time: 96.3 us -> 90.8 us (0.943)
  Pallas kernels: 92.7 us -> 87.4 us
    pallas_call x1, Pallas kernels: 92.7 us -> 87.4 us  [local(): pl.pallas_call(kernel, out_shape=jax.ShapeDtypeStruct((ROWS, D), BF), in_...]
where the time goes in v3:
time: 90.8 us; the launch traced here: 89.1 us
  Pallas kernels  87.4 us (96%)
  local copies, waits for them, and re-layouts  1.72 us (2%)
    pallas_call x1, Pallas kernels, local(): pl.pallas_call(kernel, out_shape=jax.ShapeDtypeStruct((ROWS, D), BF), in_...  87.4 us

profile of v3, /device:TPU:8, one launch (start us, length us, event | category | flops | bytes accessed | tf_op | source)
XLA Modules:
  0.0 89.1 jit_solution(18152727944979212497)
XLA Ops:
  0.0 87.4 %shard_map.82 = bf16[32,5120]{1,0:T(8,128)(2,1)} custom-call(bf16[3,32,5120]{2,1,0:T(8,128)(2,1)} %bitcast.4, s32[1,256]{1,0:T(1,128)} %bitcast.7, s32[16]{0:T(128)} %counts.1, bf16[512,640]{1,0:T(8,128)(2,1)} %kcache.1, bf16[512,640]{1,0:T(8,128)(2,1)} %vcache.1, bf16[40,128]{1,0:T(8,128)(2,1)} %bitcast.5, bf16[40,128]{1,0:T(8,128)(2,1)} %bitcast.6, ...), custom_call_target="tpu_custom_call" | custom-call | tf_op jit(solution)/shard_map/pallas_call | solution.py:413
  87.4 1.7 %copy.10 = bf16[32,5120]{1,0:T(8,128)(2,1)} copy(bf16[32,5120]{1,0:T(8,128)(2,1)} %shard_map.82) | data formatting | bytes 655360

commit v4 on v3

--- a/solution.py
+++ b/solution.py
@@ -25,14 +25,12 @@
 CH = 128
 SPAN = 512
 BASE = 192
-PIECES = ((0, 2), (2, 4), (4, 5))
+PIECES = ((0, 1), (1, 2), (2, 3), (3, 4), (4, 5))
 NP = len(PIECES)
 WIDTH = tuple((last - first) * HEAD_DIM for first, last in PIECES)
-LONG = ((0,), (1, 2))
-C1 = 3072
-C1H = C1 // 2
-C2 = D - C1
-C2H = C2 // 2
+LONG = ((0, 1), (2, 3, 4))
+XG = ((0, 1536), (1536, 1024), (2560, 512))
+YG = ((3072, 1024), (4096, 512), (4608, 512))
 SCALE2 = math.log2(math.e) / math.sqrt(HEAD_DIM)
 
 
@@ -48,9 +46,9 @@
     fresh, ridx, counts, kcache, vcache, qgain, kgain, weight, out,
     fv, gq, gk, kc, vc, wv, sent, got, sentq, gotq, selq, rbuf, kfull, vt, qs,
     of, st, so, ss, ro, rs, abuf, cat, back, att, pb,
-    rx1, ac1, ry1, sy1, ry2, sx2, rx2, ac2,
+    rx1, ac1, ry1, sy1, ry2, sx2, rx2, ac2, outv,
     lsem, qsend, qrecv, asend, arecv, rsend, rrecv, ksend, krecv, gsend, grecv,
-    dsend, drecv, tsend, trecv, usend, urecv, esend, erecv,
+    dsend, drecv, tsend, trecv, usend, urecv, esend, erecv, osem,
 ):
     j = lax.axis_index("blk")
     h = lax.axis_index("head")
@@ -121,7 +119,7 @@
         for c in range(D // HEAD_DIM):
             cols = slice(c * HEAD_DIM, (c + 1) * HEAD_DIM)
             g, i = c // NH, c % NH
-            value = (rows[:, cols] * factor * gains[c:c + 1]).astype(BF)
+            value = (rows[:, cols] * factor * gains[c:c + 1] * (SCALE2 if t == 0 else 1.0)).astype(BF)
             if t == 0:
                 p, n = piece_of(i)
                 sentq[p][g, :, n * HEAD_DIM:(n + 1) * HEAD_DIM] = value
@@ -151,7 +149,9 @@
     for load in loads[6:]:
         load.start()
     prepare(1)
+    spread(0)
     prepare(2)
+    spread(1)
 
     r_id = lax.broadcasted_iota(jnp.int32, (SPAN, CAP), 0)
     s_id = lax.broadcasted_iota(jnp.int32, (1, CAP), 1)
@@ -168,10 +168,7 @@
                 ((64, 128, 0, -1), (320, 128, 128, 1), (0, 64, 256, -2), (448, 64, 320, 2))
             )
         ])
-        if p < 2:
-            spread(p)
     back[...] = place.T
-    st[...] = jnp.zeros_like(st)
     pos = lax.broadcasted_iota(jnp.int32, (L_BLK, CAP), 0)
     hits = jnp.where(pos == jnp.where(s_id < live, ridx[...], -1), 1.0, 0.0)
     hit = jnp.sum(hits, axis=1, keepdims=True) > 0.5
@@ -202,7 +199,6 @@
         qs[p][0, 64:128] = (mine[64:128] + rbuf[p][256:320].astype(F32)).astype(BF)
         gather_send(0, 1, p)
         gather_send(1, 1, p)
-    gather_step(2)
 
     for t in range(2):
         for copy in a_copies[t]:
@@ -222,41 +218,38 @@
             query = query[0] if len(slots) == 1 else jnp.concatenate(query, axis=0)
             s0 = nt(kfull[0, :, cols], query)
             s1 = nt(kfull[1, :, cols], query)
-            top = jnp.maximum(jnp.max(s0, axis=0, keepdims=True), jnp.max(s1, axis=0, keepdims=True)) * SCALE2
-            p0 = jnp.exp2(s0 * SCALE2 - top)
-            p1 = jnp.exp2(s1 * SCALE2 - top)
+            top = jnp.maximum(jnp.max(s0, axis=0, keepdims=True), jnp.max(s1, axis=0, keepdims=True))
+            p0 = jnp.exp2(s0 - top)
+            p1 = jnp.exp2(s1 - top)
             total = jnp.sum(p0, axis=0, keepdims=True) + jnp.sum(p1, axis=0, keepdims=True)
             o = mm(vt[0, cols, :], p0.astype(BF)) + mm(vt[1, cols, :], p1.astype(BF))
             for n, s in enumerate(slots):
                 lanes = slice(n * CH, (n + 1) * CH)
                 of[s, cols, :] = o[:, lanes]
-                st[s, p, k:k + 1, :] = top[:, lanes]
-                st[s, p, 4 + k:5 + k, :] = total[:, lanes]
-
-    gather_step(3)
+                st[s, i, 0:1, :] = top[:, lanes]
+                st[s, i, 1:2, :] = total[:, lanes]
+
+    gather_step(2)
     k_copy.wait_recv()
     v_copy.wait_recv()
-    attend((7, 1), range(3))
+    attend((0,), range(NH))
+    attend((7, 1), range(2))
+    gather_step(3)
+    attend((7, 1), range(2, NH))
+    attend((6, 2), range(2))
     gather_step(4)
-    attend((7, 1), range(3, NH))
-    attend((6, 2), range(NH))
-
-    def joined(slot, p, arrivals):
-        first, last = PIECES[p]
-        tops = [st[slot, p, 0:4]] + [rs[way, step, p, 0:4] for way, step in arrivals]
-        sums = [st[slot, p, 4:8]] + [rs[way, step, p, 4:8] for way, step in arrivals]
+
+    def joined(slot, i, arrivals):
+        rows = slice(i * HEAD_DIM, (i + 1) * HEAD_DIM)
+        tops = [st[slot, i, 0:1]] + [rs[way, step, i, 0:1] for way, step in arrivals]
+        sums = [st[slot, i, 1:2]] + [rs[way, step, i, 1:2] for way, step in arrivals]
         top = functools.reduce(jnp.maximum, tops)
         factors = [jnp.exp2(t - top) for t in tops]
         total = sum(a * f for a, f in zip(sums, factors))
-        values = []
-        for i in range(first, last):
-            rows = slice(i * HEAD_DIM, (i + 1) * HEAD_DIM)
-            k = i - first
-            value = of[slot, rows, :] * factors[0][k:k + 1]
-            for n, (way, step) in enumerate(arrivals):
-                value = value + ro[way, step, rows, :].astype(F32) * factors[n + 1][k:k + 1]
-            values.append(value)
-        return values, top, total
+        value = of[slot, rows, :] * factors[0]
+        for n, (way, step) in enumerate(arrivals):
+            value = value + ro[way, step, rows, :].astype(F32) * factors[n + 1]
+        return value, top, total
 
     d_copies = {}
 
@@ -264,54 +257,58 @@
         ahead = 5 - step
         slot = ahead if way == 0 else 8 - ahead
         first, last = PIECES[p]
-        if step > (1 if p in LONG[way] else 2):
+        chained = step > (1 if p in LONG[way] else 2)
+        if chained:
             for copy in d_copies[way, step - 1, p]:
                 copy.wait_recv()
-            values, top, total = joined(slot, p, [(way, step - 2)])
-        else:
-            values = [of[slot, i * HEAD_DIM:(i + 1) * HEAD_DIM, :] for i in range(first, last)]
-            top, total = st[slot, p, 0:4], st[slot, p, 4:8]
-        for n, value in enumerate(values):
-            i = first + n
-            so[way, step - 1, i * HEAD_DIM:(i + 1) * HEAD_DIM, :] = value.astype(BF)
-        ss[way, step - 1, p, 0:4] = top
-        ss[way, step - 1, p, 4:8] = total
+        for i in range(first, last):
+            rows = slice(i * HEAD_DIM, (i + 1) * HEAD_DIM)
+            if chained:
+                value, top, total = joined(slot, i, [(way, step - 2)])
+            else:
+                value, top, total = of[slot, rows, :], st[slot, i, 0:1], st[slot, i, 1:2]
+            so[way, step - 1, rows, :] = value.astype(BF)
+            ss[way, step - 1, i, 0:1] = top
+            ss[way, step - 1, i, 1:2] = total
         rows = pl.ds(first * HEAD_DIM, WIDTH[p])
+        heads = pl.ds(first, last - first)
         dev = blk_at(2 if way == 0 else -2)
         d_copies[way, step, p] = [
-            send(ss.at[way, step - 1, p], rs.at[way, step - 1, p],
+            send(ss.at[way, step - 1, heads], rs.at[way, step - 1, heads],
                  tsend.at[way, step - 1, p], trecv.at[way, step - 1, p], dev),
             send(so.at[way, step - 1, rows], ro.at[way, step - 1, rows],
                  dsend.at[way, step - 1, p], drecv.at[way, step - 1, p], dev),
         ]
 
+    for way in range(2):
+        for p in LONG[1 - way]:
+            attend((5, 3), range(*PIECES[p]))
+            give(way, 2, p)
     for p in range(NP):
         way = 0 if p in LONG[0] else 1
         g_copies[way, 4, p].wait_recv()
         attend((4,), range(*PIECES[p]))
         give(way, 1, p)
-    for way in range(2):
-        for p in LONG[1 - way]:
-            attend((5, 3), range(*PIECES[p]))
-            give(way, 2, p)
+    attend((6, 2), range(2, NH))
     for way in range(2):
         for p in LONG[way]:
             give(way, 2, p)
-    attend((0,), range(NH))
-    order = ((0, 1), (1, 0), (0, 2), (0, 0), (1, 1), (1, 2))
+    order = (LONG[1] + LONG[0], LONG[0] + LONG[1])
     for step in (3, 4):
-        for way, p in order:
-            give(way, step, p)
+        for both in zip(*order):
+            for way in range(2):
+                give(way, step, both[way])
+    last_in = sorted(range(NP), key=lambda p: max(order[0].index(p), order[1].index(p)))
 
     u_copies = {}
-    for p in (1, 0, 2):
+    for p in last_in:
         for way in range(2):
             for copy in d_copies[way, 4, p]:
                 copy.wait_recv()
-        values, _, total = joined(0, p, [(0, 3), (1, 3)])
-        for n, value in enumerate(values):
-            result = (value / total[n:n + 1]).T.astype(BF)
-            abuf[p][:, n * HEAD_DIM:(n + 1) * HEAD_DIM] = result
+        for i in range(*PIECES[p]):
+            value, _, total = joined(0, i, [(0, 3), (1, 3)])
+            n = i - PIECES[p][0]
+            abuf[p][:, n * HEAD_DIM:(n + 1) * HEAD_DIM] = (value / total).T.astype(BF)
         u_copies[p] = [
             send(abuf[p].at[pl.ds(first, size)], cat[p].at[pl.ds(to, size)],
                  usend.at[p, n], urecv.at[p, n], blk_at(offset))
@@ -320,7 +317,7 @@
             )
         ]
         cat[p][192:320] = abuf[p][...]
-    for p in (1, 0, 2):
+    for p in last_in:
         for copy in u_copies[p]:
             copy.wait_recv()
         first = PIECES[p][0] * HEAD_DIM
@@ -339,64 +336,121 @@
     up, down, far = lax.rem(x + 1, 4), lax.rem(x + 3, 4), lax.rem(x + 2, 4)
     to_up, to_down = {"head": up * 2 + y}, {"head": down * 2 + y}
     to_pair = {"head": x * 2 + 1 - y}
-    a1, b1 = pl.ds(0, C1H), pl.ds(C1H, C1H)
-    a2, b2 = pl.ds(C1, C2H), pl.ds(C1 + C2H, C2H)
-
-    project(0, C1H)
     e = {}
-    e["p1"] = send(pb.at[far, :, :, a1], rx1.at[0], esend.at[0], erecv.at[0], to_up)
-    e["m2"] = send(pb.at[down, :, :, a1], rx1.at[1], esend.at[1], erecv.at[1], to_down)
-    project(C1, C1 + C2H)
-    e["y2"] = send(pb.at[:, 1 - y, :, a2], ry2.at[:, :, 0:C2H], esend.at[2], erecv.at[2], to_pair)
-    project(C1H, C1)
-    e["m1"] = send(pb.at[far, :, :, b1], rx1.at[2], esend.at[3], erecv.at[3], to_down)
-    e["p2"] = send(pb.at[up, :, :, b1], rx1.at[3], esend.at[4], erecv.at[4], to_up)
-    project(C1 + C2H, D)
-    e["y3"] = send(pb.at[:, 1 - y, :, b2], ry2.at[:, :, C2H:C2], esend.at[14], erecv.at[14], to_pair)
-
-    e["p1"].wait_recv()
-    ac1[0] = (rx1[0].astype(F32) + pb[up, :, :, 0:C1H].astype(F32)).astype(BF)
-    e["p3"] = send(ac1.at[0], rx1.at[4], esend.at[5], erecv.at[5], to_up)
-    e["m1"].wait_recv()
-    ac1[1] = (rx1[2].astype(F32) + pb[down, :, :, C1H:C1].astype(F32)).astype(BF)
-    e["m3"] = send(ac1.at[1], rx1.at[5], esend.at[6], erecv.at[6], to_down)
-
-    e["y2"].wait_recv()
-    e["y3"].wait_recv()
-    for i in range(4):
-        sx2[i] = (ry2[i].astype(F32) + pb[i, y, :, C1:D].astype(F32)).astype(BF)
-    a2, b2 = pl.ds(0, C2H), pl.ds(C2H, C2H)
-    e["P1"] = send(sx2.at[far, :, a2], rx2.at[0], esend.at[7], erecv.at[7], to_up)
-    e["M1"] = send(sx2.at[far, :, b2], rx2.at[2], esend.at[8], erecv.at[8], to_down)
-    e["M2"] = send(sx2.at[down, :, a2], rx2.at[1], esend.at[9], erecv.at[9], to_down)
-    e["P2"] = send(sx2.at[up, :, b2], rx2.at[3], esend.at[10], erecv.at[10], to_up)
-
-    def five(own, one, two):
-        return own.astype(F32) + one.astype(F32) + two.astype(F32)
-
-    for name in ("m2", "p2", "p3", "m3"):
-        e[name].wait_recv()
-    sy1[:, 0:C1H] = five(pb[x, 1 - y, :, 0:C1H], rx1[4, 1 - y], rx1[1, 1 - y]).astype(BF)
-    sy1[:, C1H:C1] = five(pb[x, 1 - y, :, C1H:C1], rx1[5, 1 - y], rx1[3, 1 - y]).astype(BF)
-    e["y1"] = send(sy1, ry1, esend.at[11], erecv.at[11], to_pair)
-
-    e["P1"].wait_recv()
-    ac2[0] = (rx2[0].astype(F32) + sx2[up, :, 0:C2H].astype(F32)).astype(BF)
-    e["P3"] = send(ac2.at[0], rx2.at[4], esend.at[12], erecv.at[12], to_up)
-    e["M1"].wait_recv()
-    ac2[1] = (rx2[2].astype(F32) + sx2[down, :, C2H:C2].astype(F32)).astype(BF)
-    e["M3"] = send(ac2.at[1], rx2.at[5], esend.at[13], erecv.at[13], to_down)
-
-    e["y1"].wait_recv()
-    own_a = five(pb[x, y, :, 0:C1H], rx1[4, y], rx1[1, y])
-    out[:, 0:C1H] = (own_a + ry1[:, 0:C1H].astype(F32)).astype(BF)
-    own_b = five(pb[x, y, :, C1H:C1], rx1[5, y], rx1[3, y])
-    out[:, C1H:C1] = (own_b + ry1[:, C1H:C1].astype(F32)).astype(BF)
-    for name in ("M2", "P2", "P3", "M3"):
-        e[name].wait_recv()
-    out[:, C1:C1 + C2H] = five(sx2[x, :, 0:C2H], rx2[4], rx2[1]).astype(BF)
-    out[:, C1 + C2H:D] = five(sx2[x, :, C2H:C2], rx2[5], rx2[3]).astype(BF)
-
+    stores = []
+
+    def give_sum(kind, g, n, src, dst, dev):
+        e[kind, g, n] = send(src, dst, esend.at[kind, g, n], erecv.at[kind, g, n], dev)
+
+    def arrived(kind, g, *names):
+        for n in names:
+            e[kind, g, n].wait_recv()
+
+    def ring_start(kind, g, part, dst, first, half):
+        a, b = pl.ds(first, half), pl.ds(first + half, half)
+        give_sum(kind, g, 0, part(far, a), dst.at[0], to_up)
+        give_sum(kind, g, 2, part(far, b), dst.at[2], to_down)
+        give_sum(kind, g, 1, part(down, a), dst.at[1], to_down)
+        give_sum(kind, g, 3, part(up, b), dst.at[3], to_up)
+
+    def ring_pass(kind, g, load, dst, total, first, half):
+        for n, other, cols, dev in ((0, up, first, to_up), (2, down, first + half, to_down)):
+            arrived(kind, g, n)
+            total[n // 2] = (dst[n].astype(F32) + load(other, slice(cols, cols + half)).astype(F32)).astype(BF)
+            give_sum(kind, g, 4 + n // 2, total.at[n // 2], dst.at[4 + n // 2], dev)
+
+    def add(*terms):
+        return functools.reduce(jnp.add, [t.astype(F32) for t in terms])
+
+    def store(cols):
+        copy = pltpu.make_async_copy(outv.at[:, cols], out.at[:, cols], osem.at[len(stores)])
+        copy.start()
+        stores.append(copy)
+
+    def x_start(g):
+        first, width = XG[g]
+        project(first, first + width)
+        ring_start(0, g, lambda to, cols: pb.at[to, :, :, cols], rx1[g], first, width // 2)
+
+    def x_pass(g):
+        first, width = XG[g]
+        ring_pass(0, g, lambda to, cols: pb[to, :, :, cols], rx1[g], ac1[g], first, width // 2)
+
+    def x_sums(g, row):
+        first, width = XG[g]
+        half = width // 2
+        return (
+            add(pb[x, row, :, first:first + half], rx1[g][4, row], rx1[g][1, row]),
+            add(pb[x, row, :, first + half:first + width], rx1[g][5, row], rx1[g][3, row]),
+        )
+
+    def x_turn(g):
+        half = XG[g][1] // 2
+        arrived(0, g, 1, 3, 4, 5)
+        one, two = x_sums(g, 1 - y)
+        sy1[g][:, 0:half] = one.astype(BF)
+        sy1[g][:, half:2 * half] = two.astype(BF)
+        give_sum(0, g, 6, sy1[g], ry1[g], to_pair)
+
+    def x_end(g):
+        first, width = XG[g]
+        half = width // 2
+        arrived(0, g, 6)
+        one, two = x_sums(g, y)
+        outv[:, first:first + half] = add(one, ry1[g][:, 0:half]).astype(BF)
+        outv[:, first + half:first + width] = add(two, ry1[g][:, half:width]).astype(BF)
+        store(pl.ds(first, width))
+
+    def y_start(g):
+        first, width = YG[g]
+        project(first, first + width)
+        give_sum(1, g, 6, pb.at[:, 1 - y, :, pl.ds(first, width)], ry2[g], to_pair)
+
+    def y_turn(g):
+        first, width = YG[g]
+        arrived(1, g, 6)
+        for i in range(4):
+            sx2[g][i] = add(ry2[g][i], pb[i, y, :, first:first + width]).astype(BF)
+        ring_start(1, g, lambda to, cols: sx2[g].at[to, :, cols], rx2[g], 0, width // 2)
+
+    def y_pass(g):
+        ring_pass(1, g, lambda to, cols: sx2[g][to, :, cols], rx2[g], ac2[g], 0, YG[g][1] // 2)
+
+    def y_end(g):
+        first, width = YG[g]
+        half = width // 2
+        arrived(1, g, 1, 3, 4, 5)
+        outv[:, first:first + half] = add(sx2[g][x, :, 0:half], rx2[g][4], rx2[g][1]).astype(BF)
+        outv[:, first + half:first + width] = add(sx2[g][x, :, half:width], rx2[g][5], rx2[g][3]).astype(BF)
+        store(pl.ds(first, width))
+
+    y_start(0)
+    x_start(0)
+    x_start(1)
+    y_start(1)
+    x_start(2)
+    y_start(2)
+    x_pass(0)
+    y_turn(0)
+    x_pass(1)
+    x_turn(0)
+    x_pass(2)
+    y_turn(1)
+    y_pass(0)
+    x_turn(1)
+    y_turn(2)
+    x_turn(2)
+    y_pass(1)
+    y_pass(2)
+    x_end(0)
+    y_end(0)
+    x_end(1)
+    y_end(1)
+    x_end(2)
+    y_end(2)
+
+    for copy in stores:
+        copy.wait()
     for copy in pending:
         copy.wait_send()
 
@@ -414,27 +468,28 @@
         kernel,
         out_shape=jax.ShapeDtypeStruct((ROWS, D), BF),
         in_specs=[any_spec, vmem, pl.BlockSpec(memory_space=pltpu.SMEM)] + [any_spec] * 5,
-        out_specs=vmem,
+        out_specs=any_spec,
         scratch_shapes=[
             V((3, ROWS, D), BF), V((D // 128, 128), BF), V((D // 128, 128), BF),
             V((L_BLK, GROUP), BF), V((L_BLK, GROUP), BF), V((GROUP, D), BF),
             V((2, NG, ROWS, GROUP), BF), V((2, CAP, GROUP), BF),
             by_piece(NG, ROWS), by_piece(CAP), by_piece(SPAN), by_piece(384),
             V((2, L_BLK, GROUP), BF), V((2, GROUP, L_BLK), BF), by_piece(8, CH),
-            V((8, GROUP, CH), F32), V((8, NP, 8, CH), F32),
-            V((2, 4, GROUP, CH), BF), V((2, 4, NP, 8, CH), F32),
-            V((2, 4, GROUP, CH), BF), V((2, 4, NP, 8, CH), F32),
+            V((8, GROUP, CH), F32), V((8, NH, 2, CH), F32),
+            V((2, 4, GROUP, CH), BF), V((2, 4, NH, 2, CH), F32),
+            V((2, 4, GROUP, CH), BF), V((2, 4, NH, 2, CH), F32),
             by_piece(CH), by_piece(SPAN), V((CAP, SPAN), BF), V((CAP, GROUP), BF),
             V((4, 2, ROWS, D), BF),
-            V((6, 2, ROWS, C1H), BF), V((2, 2, ROWS, C1H), BF),
-            V((ROWS, C1), BF), V((ROWS, C1), BF),
-            V((4, ROWS, C2), BF), V((4, ROWS, C2), BF),
-            V((6, ROWS, C2H), BF), V((2, ROWS, C2H), BF),
+            [V((6, 2, ROWS, w // 2), BF) for _, w in XG], [V((2, 2, ROWS, w // 2), BF) for _, w in XG],
+            [V((ROWS, w), BF) for _, w in XG], [V((ROWS, w), BF) for _, w in XG],
+            [V((4, ROWS, w), BF) for _, w in YG], [V((4, ROWS, w), BF) for _, w in YG],
+            [V((6, ROWS, w // 2), BF) for _, w in YG], [V((2, ROWS, w // 2), BF) for _, w in YG],
+            V((ROWS, D), BF),
             dma((8,)), dma((NP, 7)), dma((NP, 7)), dma((2, 7)), dma((2, 7)),
             dma((NP, 4)), dma((NP, 4)), dma((2,)), dma((2,)),
             dma((2, 4, NP)), dma((2, 4, NP)),
             dma((2, 4, NP)), dma((2, 4, NP)), dma((2, 4, NP)), dma((2, 4, NP)),
-            dma((NP, 4)), dma((NP, 4)), dma((15,)), dma((15,)),
+            dma((NP, 4)), dma((NP, 4)), dma((2, 3, 7)), dma((2, 3, 7)), dma((6,)),
         ],
         compiler_params=pltpu.CompilerParams(
             collective_id=0, has_side_effects=True, vmem_limit_bytes=56 * 1024 * 1024

time: 90.8 us -> 90.1 us (level); the launches traced: 89.1 us -> 89.7 us
  no operation moved by 1% of the time
where the time goes in v4:
time: 90.1 us; the launch traced here: 89.7 us
  Pallas kernels  88 us (98%)
  local copies, waits for them, and re-layouts  1.72 us (2%)
    pallas_call x1, Pallas kernels, local(): pl.pallas_call(kernel, out_shape=jax.ShapeDtypeStruct((ROWS, D), BF), in_...  88 us

profile of v4, /device:TPU:8, one launch (start us, length us, event | category | flops | bytes accessed | tf_op | source)
XLA Modules:
  0.0 89.7 jit_solution(1315673030963827467)
XLA Ops:
  0.0 88.0 %shard_map.82 = bf16[32,5120]{1,0:T(8,128)(2,1)} custom-call(bf16[3,32,5120]{2,1,0:T(8,128)(2,1)} %bitcast.4, s32[1,256]{1,0:T(1,128)} %bitcast.7, s32[16]{0:T(128)} %counts.1, bf16[512,640]{1,0:T(8,128)(2,1)} %kcache.1, bf16[512,640]{1,0:T(8,128)(2,1)} %vcache.1, bf16[40,128]{1,0:T(8,128)(2,1)} %bitcast.5, bf16[40,128]{1,0:T(8,128)(2,1)} %bitcast.6, ...), custom_call_target="tpu_custom_call" | custom-call | tf_op jit(solution)/shard_map/pallas_call | solution.py:467
  88.0 1.7 %copy.10 = bf16[32,5120]{1,0:T(8,128)(2,1)} copy(bf16[32,5120]{1,0:T(8,128)(2,1)} %shard_map.82) | data formatting | bytes 655360

commit v5 on v4

v5 whole, which is shorter than its diff:
```python
import functools
import math

import jax
import jax.numpy as jnp
from jax import lax
from jax.experimental import pallas as pl
from jax.experimental.pallas import tpu as pltpu
from jax.sharding import PartitionSpec as P

HEAD_DIM = 128
EPS = 1e-06
MESH = pl.DeviceIdType.MESH
BF = jnp.bfloat16
F32 = jnp.float32

D = 5120
GROUP = 640
NH = GROUP // HEAD_DIM
NG = 8
NB = 16
CAP = 256
L_BLK = 512
ROWS = 32
CH = 128
SPAN = 512
BASE = 192
NP = NH
LONG = ((0, 1), (2, 3, 4))
XG = ((0, 1024), (1024, 1536), (2560, 512))
YG = ((3072, 1536), (4608, 512))
SCALE2 = math.log2(math.e) / math.sqrt(HEAD_DIM)


def nt(a, b):
    return lax.dot_general(a, b, (((1,), (1,)), ((), ())), preferred_element_type=F32)


def mm(a, b):
    return jnp.dot(a, b, preferred_element_type=F32)


def kernel(
    fresh, ridx, counts, kcache, vcache, qgain, kgain, weight, out,
    fv, gq, gk, kc, vc, wv, sent, got, sentq, gotq, selq, rbuf, kfull, vt, qs,
    of, st, so, ss, ro, rs, abuf, cat, back, att, pb,
    rx1, ac1, ry1, sy1, ry2, sx2, rx2, ac2, outv,
    unit, lsem, ssem, qrecv, arecv, rrecv, krecv, grecv, drecv, urecv, erecv, osem,
):
    j = lax.axis_index("blk")
    h = lax.axis_index("head")
    core = lax.rem(j, 2)
    x, y = lax.div(h, 2), lax.rem(h, 2)

    def blk_at(offset):
        return {"blk": lax.rem(j + offset + NB, NB)}

    sibling = {"blk": j + 1 - 2 * core}

    def head_at(dx, dy):
        other_y = 1 - y if dy else y
        return lax.rem(x + dx, 4) * 2 + other_y

    def send(src, dst, phase, r, dev):
        pltpu.make_async_remote_copy(
            src_ref=src, dst_ref=dst, send_sem=ssem.at[phase], recv_sem=r, device_id=dev, device_id_type=MESH
        ).start()

    def landed(like, sem):
        pltpu.make_async_copy(like, like, sem).wait()

    loads = [
        pltpu.make_async_copy(src, dst, lsem.at[i])
        for i, (src, dst) in enumerate((
            (fresh.at[0], fv.at[0]), (qgain, gq), (fresh.at[1], fv.at[1]), (kgain, gk),
            (fresh.at[2], fv.at[2]), (kcache, kc), (vcache, vc), (weight, wv),
        ))
    ]
    for load in loads[:6]:
        load.start()

    barrier = pltpu.get_barrier_semaphore()
    pairs = [(2, 1), (1, 1), (3, 1), (2, 0), (0, 1), (1, 0), (3, 0)]
    for dx, dy in pairs:
        pl.semaphore_signal(barrier, inc=1, device_id={"head": head_at(dx, dy)}, device_id_type=MESH)
    for offset in (-2, -1, 1, 2):
        pl.semaphore_signal(barrier, inc=1, device_id=blk_at(offset), device_id_type=MESH)

    live = counts[j]
    before = jnp.int32(0)
    for i in range(NB):
        before = before + jnp.where(i < j, counts[i], 0)
    shift = before - CH * j + BASE

    my_rows = pl.ds(pl.multiple_of(h * ROWS, ROWS), ROWS)

    def prepare(t):
        loads[2 * t].wait()
        if t == 2:
            for g in range(NG):
                sent[1, g] = fv[t, :, g * GROUP:(g + 1) * GROUP]
            got[1, my_rows] = sent[1, h]
            return
        loads[2 * t + 1].wait()
        rows = fv[t].astype(F32)
        factor = lax.rsqrt(jnp.mean(rows * rows, axis=-1, keepdims=True) + EPS)
        gains = (gq if t == 0 else gk)[...].astype(F32)
        for c in range(D // HEAD_DIM):
            cols = slice(c * HEAD_DIM, (c + 1) * HEAD_DIM)
            g, i = c // NH, c % NH
            value = (rows[:, cols] * factor * gains[c:c + 1] * (SCALE2 if t == 0 else 1.0)).astype(BF)
            if t == 0:
                sentq[i][g] = value
            else:
                sent[0, g, :, i * HEAD_DIM:(i + 1) * HEAD_DIM] = value
        if t == 0:
            for p in range(NP):
                gotq[p][my_rows] = sentq[p][h]
        else:
            got[0, my_rows] = sent[0, h]

    def spread(t):
        for dx, dy in pairs:
            peer = head_at(dx, dy)
            send(sent.at[t, peer], got.at[t, my_rows], 1, arecv.at[t], {"head": peer})

    prepare(0)
    pl.semaphore_wait(barrier, len(pairs) + 4)
    for p in range(NP):
        for dx, dy in pairs:
            peer = head_at(dx, dy)
            send(sentq[p].at[peer], gotq[p].at[my_rows], 0, qrecv.at[p], {"head": peer})
    for load in loads[6:]:
        load.start()
    prepare(1)
    spread(0)
    prepare(2)
    spread(1)

    r_id = lax.broadcasted_iota(jnp.int32, (SPAN, CAP), 0)
    s_id = lax.broadcasted_iota(jnp.int32, (1, CAP), 1)
    place = jnp.where(r_id == jnp.where(s_id < live, s_id + shift, -1), 1.0, 0.0).astype(BF)
    for p in range(NP):
        landed(gotq[p].at[0:CAP - ROWS], qrecv.at[p])
        selq[p][...] = mm(place, gotq[p][...]).astype(BF)
        for first, size, to, offset in ((64, 128, 0, -1), (320, 128, 128, 1), (0, 64, 256, -2), (448, 64, 320, 2)):
            send(selq[p].at[pl.ds(first, size)], rbuf[p].at[pl.ds(to, size)], 2, rrecv.at[p], blk_at(offset))
    back[...] = place.T
    pos = lax.broadcasted_iota(jnp.int32, (L_BLK, CAP), 0)
    hits = jnp.where(pos == jnp.where(s_id < live, ridx[...], -1), 1.0, 0.0)
    hit = jnp.sum(hits, axis=1, keepdims=True) > 0.5
    hits = hits.astype(BF)

    def gather_send(way, step, p):
        src = (8 - (step - 1)) % 8 if way == 0 else step - 1
        dst = 8 - step if way == 0 else step
        send(qs[p].at[src], qs[p].at[dst], 4, grecv.at[way, step - 1, p], blk_at(2 if way == 0 else -2))

    def gathered(way, step, p):
        landed(qs[p].at[0], grecv.at[way, step - 1, p])

    def gather_step(step, p):
        for way in range(2):
            gathered(way, step - 1, p)
            if step < 4 or p in LONG[way]:
                gather_send(way, step, p)

    for p in range(NP):
        landed(rbuf[p], rrecv.at[p])
        mine = (selq[p][192:320].astype(F32) + rbuf[p][0:128].astype(F32)) + rbuf[p][128:256].astype(F32)
        qs[p][0, 0:64] = (mine[0:64] + rbuf[p][320:384].astype(F32)).astype(BF)
        qs[p][0, 64:128] = (mine[64:128] + rbuf[p][256:320].astype(F32)).astype(BF)
        gather_send(0, 1, p)
        gather_send(1, 1, p)

    for t in range(2):
        landed(got.at[t, 0:CAP - ROWS], arecv.at[t])
    loads[5].wait()
    loads[6].wait()
    kfull[0] = jnp.where(hit, mm(hits, got[0]), kc[...].astype(F32)).astype(BF)
    send(kfull.at[0], kfull.at[1], 3, krecv.at[0], sibling)
    vt[0] = jnp.where(hit, mm(hits, got[1]), vc[...].astype(F32)).T.astype(BF)
    send(vt.at[0], vt.at[1], 3, krecv.at[1], sibling)

    def attend(slots, need=None, done=None):
        def scores(i, b):
            query = [qs[i][s] for s in slots]
            query = query[0] if len(slots) == 1 else jnp.concatenate(query, axis=0)
            cols = slice(i * HEAD_DIM, (i + 1) * HEAD_DIM)
            return nt(kfull[b // 2, b % 2 * 256:b % 2 * 256 + 256, cols], query)

        def weighted(i, b, weights):
            return mm(vt[b // 2, i * HEAD_DIM:(i + 1) * HEAD_DIM, b % 2 * 256:b % 2 * 256 + 256], weights)

        def keep(i, value):
            for n, s in enumerate(slots):
                of[s, i * HEAD_DIM:(i + 1) * HEAD_DIM, :] = value[:, n * CH:(n + 1) * CH]
            if done is not None:
                done(i)

        if need is not None:
            need(0)
        now = [scores(0, b) for b in range(4)]
        last = []
        for i in range(NH):
            top = functools.reduce(jnp.maximum, [jnp.max(block, axis=0, keepdims=True) for block in now])
            if i + 1 < NH and need is not None:
                need(i + 1)
            ahead, weights, total, value = [], [], 0.0, 0.0
            for b in range(4):
                if i + 1 < NH:
                    ahead.append(scores(i + 1, b))
                one = jnp.exp2(now[b] - top)
                total = total + jnp.sum(one, axis=0, keepdims=True)
                weights.append(one.astype(BF))
                if i:
                    value = value + weighted(i - 1, b, last[b])
            for n, s in enumerate(slots):
                st[s, i, 0:1, :] = top[:, n * CH:(n + 1) * CH]
                st[s, i, 1:2, :] = total[:, n * CH:(n + 1) * CH]
            if i:
                keep(i - 1, value)
            now, last = ahead, weights
        value = functools.reduce(jnp.add, [weighted(NH - 1, b, last[b]) for b in range(4)])
        keep(NH - 1, value)

    for p in range(NP):
        gather_step(2, p)
    landed(kfull.at[1], krecv.at[0])
    landed(vt.at[1], krecv.at[1])
    attend((0, 7, 1), need=functools.partial(gather_step, 3))
    attend((6, 2), need=functools.partial(gather_step, 4))

    def joined(slot, i, arrivals):
        rows = slice(i * HEAD_DIM, (i + 1) * HEAD_DIM)
        tops = [st[slot, i, 0:1]] + [rs[way, step, i, 0:1] for way, step in arrivals]
        sums = [st[slot, i, 1:2]] + [rs[way, step, i, 1:2] for way, step in arrivals]
        top = functools.reduce(jnp.maximum, tops)
        factors = [jnp.exp2(t - top) for t in tops]
        total = sum(a * f for a, f in zip(sums, factors))
        value = of[slot, rows, :] * factors[0]
        for n, (way, step) in enumerate(arrivals):
            value = value + ro[way, step, rows, :].astype(F32) * factors[n + 1]
        return value, top, total

    def give(way, step, p):
        ahead = 5 - step
        slot = ahead if way == 0 else 8 - ahead
        rows = slice(p * HEAD_DIM, (p + 1) * HEAD_DIM)
        if step > (1 if p in LONG[way] else 2):
            landed(unit.at[0:33], drecv.at[way, step - 2, p])
            value, top, total = joined(slot, p, [(way, step - 2)])
        else:
            value, top, total = of[slot, rows, :], st[slot, p, 0:1], st[slot, p, 1:2]
        so[way, step - 1, rows, :] = value.astype(BF)
        ss[way, step - 1, p, 0:1] = top
        ss[way, step - 1, p, 1:2] = total
        rows = pl.ds(p * HEAD_DIM, HEAD_DIM)
        dev = blk_at(2 if way == 0 else -2)
        send(ss.at[way, step - 1, p], rs.at[way, step - 1, p], 6, drecv.at[way, step - 1, p], dev)
        send(so.at[way, step - 1, rows], ro.at[way, step - 1, rows], 5, drecv.at[way, step - 1, p], dev)

    def long_way(p):
        return 0 if p in LONG[0] else 1

    attend((5, 3), done=lambda p: give(1 - long_way(p), 2, p))
    attend((4,), need=lambda p: gathered(long_way(p), 4, p), done=lambda p: give(long_way(p), 1, p))
    for p in range(NP):
        give(long_way(p), 2, p)
    order = (LONG[1] + LONG[0], LONG[0] + LONG[1])
    for step in (3, 4):
        for both in zip(*order):
            for way in range(2):
                give(way, step, both[way])
    last_in = sorted(range(NP), key=lambda p: max(order[0].index(p), order[1].index(p)))

    for p in last_in:
        for way in range(2):
            landed(unit.at[0:33], drecv.at[way, 3, p])
        value, _, total = joined(0, p, [(0, 3), (1, 3)])
        abuf[p][...] = (value / total).T.astype(BF)
        for first, size, to, offset in ((0, 128, 320, -1), (0, 128, 64, 1), (0, 64, 448, -2), (64, 64, 0, 2)):
            send(abuf[p].at[pl.ds(first, size)], cat[p].at[pl.ds(to, size)], 7, urecv.at[p], blk_at(offset))
        cat[p][192:320] = abuf[p][...]
    for p in last_in:
        landed(rbuf[p], urecv.at[p])
        att[:, p * HEAD_DIM:(p + 1) * HEAD_DIM] = mm(back[...], cat[p][...]).astype(BF)

    loads[7].wait()

    def project(first, last):
        for at in range(first, last, 512):
            cols = slice(at, at + 512)
            tile = mm(att[...], wv[:, cols]).astype(BF)
            for g in range(NG):
                pb[g // 2, g % 2, :, cols] = tile[g * ROWS:(g + 1) * ROWS]

    up, down, far = lax.rem(x + 1, 4), lax.rem(x + 3, 4), lax.rem(x + 2, 4)
    to_up, to_down = {"head": up * 2 + y}, {"head": down * 2 + y}
    to_pair = {"head": x * 2 + 1 - y}
    stores = []

    def give_sum(kind, g, n, src, dst, dev):
        send(src, dst, 8, erecv.at[kind, g, (0, 2, 1, 2, 2, 2, 3)[n]], dev)

    def ring_start(kind, g, part, dst, first, half):
        a, b = pl.ds(first, half), pl.ds(first + half, half)
        give_sum(kind, g, 0, part(far, a), dst.at[0], to_up)
        give_sum(kind, g, 2, part(far, b), dst.at[2], to_down)
        give_sum(kind, g, 1, part(down, a), dst.at[1], to_down)
        give_sum(kind, g, 3, part(up, b), dst.at[3], to_up)

    def ring_pass(kind, g, load, dst, total, first, half):
        for n, other, cols, dev in ((0, up, first, to_up), (2, down, first + half, to_down)):
            landed(dst.at[n], erecv.at[kind, g, n // 2])
            total[n // 2] = (dst[n].astype(F32) + load(other, slice(cols, cols + half)).astype(F32)).astype(BF)
            give_sum(kind, g, 4 + n // 2, total.at[n // 2], dst.at[4 + n // 2], dev)

    def add(*terms):
        return functools.reduce(jnp.add, [t.astype(F32) for t in terms])

    def store(cols):
        copy = pltpu.make_async_copy(outv.at[:, cols], out.at[:, cols], osem.at[len(stores)])
        copy.start()
        stores.append(copy)

    def x_start(g):
        first, width = XG[g]
        project(first, first + width)
        ring_start(0, g, lambda to, cols: pb.at[to, :, :, cols], rx1[g], first, width // 2)

    def x_pass(g):
        first, width = XG[g]
        ring_pass(0, g, lambda to, cols: pb[to, :, :, cols], rx1[g], ac1[g], first, width // 2)

    def x_sums(g, row):
        first, width = XG[g]
        half = width // 2
        return (
            add(pb[x, row, :, first:first + half], rx1[g][4, row], rx1[g][1, row]),
            add(pb[x, row, :, first + half:first + width], rx1[g][5, row], rx1[g][3, row]),
        )

    def x_turn(g):
        half = XG[g][1] // 2
        landed(rx1[g].at[0:4], erecv.at[0, g, 2])
        one, two = x_sums(g, 1 - y)
        sy1[g][:, 0:half] = one.astype(BF)
        sy1[g][:, half:2 * half] = two.astype(BF)
        give_sum(0, g, 6, sy1[g], ry1[g], to_pair)

    def x_end(g):
        first, width = XG[g]
        half = width // 2
        landed(ry1[g], erecv.at[0, g, 3])
        one, two = x_sums(g, y)
        outv[:, first:first + half] = add(one, ry1[g][:, 0:half]).astype(BF)
        outv[:, first + half:first + width] = add(two, ry1[g][:, half:width]).astype(BF)
        store(pl.ds(first, width))

    def y_start(g):
        first, width = YG[g]
        project(first, first + width)
        give_sum(1, g, 6, pb.at[:, 1 - y, :, pl.ds(first, width)], ry2[g], to_pair)

    def y_turn(g):
        first, width = YG[g]
        landed(ry2[g], erecv.at[1, g, 3])
        for i in range(4):
            sx2[g][i] = add(ry2[g][i], pb[i, y, :, first:first + width]).astype(BF)
        ring_start(1, g, lambda to, cols: sx2[g].at[to, :, cols], rx2[g], 0, width // 2)

    def y_pass(g):
        ring_pass(1, g, lambda to, cols: sx2[g][to, :, cols], rx2[g], ac2[g], 0, YG[g][1] // 2)

    def y_end(g):
        first, width = YG[g]
        half = width // 2
        landed(rx2[g].at[0:4], erecv.at[1, g, 2])
        outv[:, first:first + half] = add(sx2[g][x, :, 0:half], rx2[g][4], rx2[g][1]).astype(BF)
        outv[:, first + half:first + width] = add(sx2[g][x, :, half:width], rx2[g][5], rx2[g][3]).astype(BF)
        store(pl.ds(first, width))

    x_start(0)
    y_start(0)
    x_start(1)
    y_start(1)
    x_start(2)
    x_pass(0)
    x_pass(1)
    y_turn(0)
    x_turn(0)
    x_pass(2)
    y_turn(1)
    x_turn(1)
    y_pass(0)
    x_turn(2)
    y_pass(1)
    x_end(0)
    x_end(1)
    y_end(0)
    x_end(2)
    y_end(1)

    for copy in stores:
        copy.wait()
    for phase, rows, cols in (
        (0, 32, 4480), (1, 64, 4480), (2, 64, 3840), (3, 128, 5120), (4, 128, 4480), (5, 128, 4480),
        (7, 64, 3840), (8, 256, 4480),
    ):
        landed(wv.at[0:rows, 0:cols], ssem.at[phase])
    landed(unit, ssem.at[6])


def local(fresh, rows_index, counts, key_cache, value_cache, q_gain, k_gain, out_weight):
    any_spec = pl.BlockSpec(memory_space=pl.ANY)
    vmem = pl.BlockSpec(memory_space=pltpu.VMEM)
    dma = pltpu.SemaphoreType.DMA
    V = pltpu.VMEM

    def by_piece(*dims):
        return [V(dims + (HEAD_DIM,), BF)] * NP

    return pl.pallas_call(
        kernel,
        out_shape=jax.ShapeDtypeStruct((ROWS, D), BF),
        in_specs=[any_spec, vmem, pl.BlockSpec(memory_space=pltpu.SMEM)] + [any_spec] * 5,
        out_specs=any_spec,
        scratch_shapes=[
            V((3, ROWS, D), BF), V((D // 128, 128), BF), V((D // 128, 128), BF),
            V((L_BLK, GROUP), BF), V((L_BLK, GROUP), BF), V((GROUP, D), BF),
            V((2, NG, ROWS, GROUP), BF), V((2, CAP, GROUP), BF),
            by_piece(NG, ROWS), by_piece(CAP), by_piece(SPAN), by_piece(384),
            V((2, L_BLK, GROUP), BF), V((2, GROUP, L_BLK), BF), by_piece(8, CH),
            V((8, GROUP, CH), F32), V((8, NH, 2, CH), F32),
            V((2, 4, GROUP, CH), BF), V((2, 4, NH, 2, CH), F32),
            V((2, 4, GROUP, CH), BF), V((2, 4, NH, 2, CH), F32),
            by_piece(CH), by_piece(SPAN), V((CAP, SPAN), BF), V((CAP, GROUP), BF),
            V((4, 2, ROWS, D), BF),
            [V((6, 2, ROWS, w // 2), BF) for _, w in XG], [V((2, 2, ROWS, w // 2), BF) for _, w in XG],
            [V((ROWS, w), BF) for _, w in XG], [V((ROWS, w), BF) for _, w in XG],
            [V((4, ROWS, w), BF) for _, w in YG], [V((4, ROWS, w), BF) for _, w in YG],
            [V((6, ROWS, w // 2), BF) for _, w in YG], [V((2, ROWS, w // 2), BF) for _, w in YG],
            V((ROWS, D), BF),
            V((35, 2, CH), F32), dma((8,)), dma((9,)), dma((NP,)), dma((2,)), dma((NP,)), dma((2,)),
            dma((2, 4, NP)), dma((2, 4, NP)), dma((NP,)), dma((2, 3, 4)), dma((5,)),
        ],
        compiler_params=pltpu.CompilerParams(
            collective_id=0, has_side_effects=True, vmem_limit_bytes=56 * 1024 * 1024
        ),
    )(
        jnp.transpose(fresh, (1, 0, 2)), rows_index.reshape(1, CAP), counts, key_cache, value_cache,
        q_gain.reshape(D // 128, 128), k_gain.reshape(D // 128, 128), out_weight,
    )


def solution(mesh):
    placed = (
        P(("cfg", "blk", "head"), None, None),
        P("blk"),
        P(),
        P(("cfg", "blk"), "head"),
        P(("cfg", "blk"), "head"),
        P(),
        P(),
        P("head", None),
    )
    return jax.shard_map(
        local,
        mesh=mesh,
        in_specs=placed,
        out_specs=P(("cfg", "blk", "head"), None),
        check_vma=False,
    )
```

time: 90.1 us -> 81 us (0.90)
  Pallas kernels: 88 us -> 78.8 us
    pallas_call x1, Pallas kernels: 88 us -> 78.8 us  [local(): pl.pallas_call(kernel, out_shape=jax.ShapeDtypeStruct((ROWS, D), BF), in_...]
where the time goes in v5:
time: 81 us; the launch traced here: 80.5 us
  Pallas kernels  78.8 us (97%)
  local copies, waits for them, and re-layouts  1.72 us (2%)
    pallas_call x1, Pallas kernels, local(): pl.pallas_call(kernel, out_shape=jax.ShapeDtypeStruct((ROWS, D), BF), in_...  78.8 us
    unnamed x1, local copies, waits for them, and re-layouts  1.72 us

profile of v5, /device:TPU:8, one launch (start us, length us, event | category | flops | bytes accessed | tf_op | source)
XLA Modules:
  0.0 80.5 jit_solution(13292444122113785701)
XLA Ops:
  0.0 78.8 %shard_map.82 = bf16[32,5120]{1,0:T(8,128)(2,1)} custom-call(bf16[3,32,5120]{2,1,0:T(8,128)(2,1)} %bitcast.4, s32[1,256]{1,0:T(1,128)} %bitcast.7, s32[16]{0:T(128)} %counts.1, bf16[512,640]{1,0:T(8,128)(2,1)} %kcache.1, bf16[512,640]{1,0:T(8,128)(2,1)} %vcache.1, bf16[40,128]{1,0:T(8,128)(2,1)} %bitcast.5, bf16[40,128]{1,0:T(8,128)(2,1)} %bitcast.6, ...), custom_call_target="tpu_custom_call" | custom-call | tf_op jit(solution)/shard_map/pallas_call | solution.py:424
  78.8 1.7 %copy.10 = bf16[32,5120]{1,0:T(8,128)(2,1)} copy(bf16[32,5120]{1,0:T(8,128)(2,1)} %shard_map.82) | data formatting | bytes 655360

commit v6 on v5

--- a/solution.py
+++ b/solution.py
@@ -154,14 +154,14 @@
     def gather_send(way, step, p):
         src = (8 - (step - 1)) % 8 if way == 0 else step - 1
         dst = 8 - step if way == 0 else step
-        send(qs[p].at[src], qs[p].at[dst], 4, grecv.at[way, step - 1, p], blk_at(2 if way == 0 else -2))
-
-    def gathered(way, step, p):
-        landed(qs[p].at[0], grecv.at[way, step - 1, p])
+        send(qs[p].at[src], qs[p].at[dst], 4, grecv.at[step - 1, p], blk_at(2 if way == 0 else -2))
+
+    def gathered(step, p):
+        landed(qs[p].at[0:2] if step < 4 else qs[p].at[0], grecv.at[step - 1, p])
 
     def gather_step(step, p):
+        gathered(step - 1, p)
         for way in range(2):
-            gathered(way, step - 1, p)
             if step < 4 or p in LONG[way]:
                 gather_send(way, step, p)
 
@@ -173,14 +173,18 @@
         gather_send(0, 1, p)
         gather_send(1, 1, p)
 
-    for t in range(2):
-        landed(got.at[t, 0:CAP - ROWS], arecv.at[t])
+    landed(got.at[0, 0:CAP - ROWS], arecv.at[0])
     loads[5].wait()
-    loads[6].wait()
     kfull[0] = jnp.where(hit, mm(hits, got[0]), kc[...].astype(F32)).astype(BF)
     send(kfull.at[0], kfull.at[1], 3, krecv.at[0], sibling)
+    for p in (0, 1):
+        gather_step(2, p)
+    landed(got.at[1, 0:CAP - ROWS], arecv.at[1])
+    loads[6].wait()
     vt[0] = jnp.where(hit, mm(hits, got[1]), vc[...].astype(F32)).T.astype(BF)
     send(vt.at[0], vt.at[1], 3, krecv.at[1], sibling)
+    for p in (2, 3, 4):
+        gather_step(2, p)
 
     def attend(slots, need=None, done=None):
         def scores(i, b):
@@ -224,11 +228,13 @@
         value = functools.reduce(jnp.add, [weighted(NH - 1, b, last[b]) for b in range(4)])
         keep(NH - 1, value)
 
-    for p in range(NP):
-        gather_step(2, p)
+    def first_needs(p):
+        gather_step(3, p)
+        if p == 2:
+            landed(vt.at[1], krecv.at[1])
+
     landed(kfull.at[1], krecv.at[0])
-    landed(vt.at[1], krecv.at[1])
-    attend((0, 7, 1), need=functools.partial(gather_step, 3))
+    attend((0, 7, 1), need=first_needs)
     attend((6, 2), need=functools.partial(gather_step, 4))
 
     def joined(slot, i, arrivals):
@@ -263,8 +269,8 @@
     def long_way(p):
         return 0 if p in LONG[0] else 1
 
+    attend((4,), need=lambda p: gathered(4, p), done=lambda p: give(long_way(p), 1, p))
     attend((5, 3), done=lambda p: give(1 - long_way(p), 2, p))
-    attend((4,), need=lambda p: gathered(long_way(p), 4, p), done=lambda p: give(long_way(p), 1, p))
     for p in range(NP):
         give(long_way(p), 2, p)
     order = (LONG[1] + LONG[0], LONG[0] + LONG[1])
@@ -298,7 +304,6 @@
     up, down, far = lax.rem(x + 1, 4), lax.rem(x + 3, 4), lax.rem(x + 2, 4)
     to_up, to_down = {"head": up * 2 + y}, {"head": down * 2 + y}
     to_pair = {"head": x * 2 + 1 - y}
-    stores = []
 
     def give_sum(kind, g, n, src, dst, dev):
         send(src, dst, 8, erecv.at[kind, g, (0, 2, 1, 2, 2, 2, 3)[n]], dev)
@@ -320,9 +325,7 @@
         return functools.reduce(jnp.add, [t.astype(F32) for t in terms])
 
     def store(cols):
-        copy = pltpu.make_async_copy(outv.at[:, cols], out.at[:, cols], osem.at[len(stores)])
-        copy.start()
-        stores.append(copy)
+        pltpu.make_async_copy(outv.at[:, cols], out.at[:, cols], osem.at[0]).start()
 
     def x_start(g):
         first, width = XG[g]
@@ -402,8 +405,7 @@
     x_end(2)
     y_end(1)
 
-    for copy in stores:
-        copy.wait()
+    landed(outv, osem.at[0])
     for phase, rows, cols in (
         (0, 32, 4480), (1, 64, 4480), (2, 64, 3840), (3, 128, 5120), (4, 128, 4480), (5, 128, 4480),
         (7, 64, 3840), (8, 256, 4480),
@@ -443,7 +445,7 @@
             [V((6, ROWS, w // 2), BF) for _, w in YG], [V((2, ROWS, w // 2), BF) for _, w in YG],
             V((ROWS, D), BF),
             V((35, 2, CH), F32), dma((8,)), dma((9,)), dma((NP,)), dma((2,)), dma((NP,)), dma((2,)),
-            dma((2, 4, NP)), dma((2, 4, NP)), dma((NP,)), dma((2, 3, 4)), dma((5,)),
+            dma((4, NP)), dma((2, 4, NP)), dma((NP,)), dma((2, 3, 4)), dma((1,)),
         ],
         compiler_params=pltpu.CompilerParams(
             collective_id=0, has_side_effects=True, vmem_limit_bytes=56 * 1024 * 1024

time: 81 us -> 80.6 us (level)
  Pallas kernels: 78.8 us -> 77.9 us
    pallas_call x1, Pallas kernels: 78.8 us -> 77.9 us  [local(): pl.pallas_call(kernel, out_shape=jax.ShapeDtypeStruct((ROWS, D), BF), in_...]
where the time goes in v6:
time: 80.6 us; the launch traced here: 79.6 us
  Pallas kernels  77.9 us (97%)
  local copies, waits for them, and re-layouts  1.72 us (2%)
    pallas_call x1, Pallas kernels, local(): pl.pallas_call(kernel, out_shape=jax.ShapeDtypeStruct((ROWS, D), BF), in_...  77.9 us
    unnamed x1, local copies, waits for them, and re-layouts  1.72 us

profile of v6, /device:TPU:8, one launch (start us, length us, event | category | flops | bytes accessed | tf_op | source)
XLA Modules:
  0.0 79.6 jit_solution(10734291965825752872)
XLA Ops:
  0.0 77.9 %shard_map.82 = bf16[32,5120]{1,0:T(8,128)(2,1)} custom-call(bf16[3,32,5120]{2,1,0:T(8,128)(2,1)} %bitcast.4, s32[1,256]{1,0:T(1,128)} %bitcast.7, s32[16]{0:T(128)} %counts.1, bf16[512,640]{1,0:T(8,128)(2,1)} %kcache.1, bf16[512,640]{1,0:T(8,128)(2,1)} %vcache.1, bf16[40,128]{1,0:T(8,128)(2,1)} %bitcast.5, bf16[40,128]{1,0:T(8,128)(2,1)} %bitcast.6, ...), custom_call_target="tpu_custom_call" | custom-call | tf_op jit(solution)/shard_map/pallas_call | solution.py:426
  77.9 1.7 %copy.10 = bf16[32,5120]{1,0:T(8,128)(2,1)} copy(bf16[32,5120]{1,0:T(8,128)(2,1)} %shard_map.82) | data formatting | bytes 655360

commit v7 on v6

--- a/solution.py
+++ b/solution.py
@@ -44,8 +44,8 @@
     fresh, ridx, counts, kcache, vcache, qgain, kgain, weight, out,
     fv, gq, gk, kc, vc, wv, sent, got, sentq, gotq, selq, rbuf, kfull, vt, qs,
     of, st, so, ss, ro, rs, abuf, cat, back, att, pb,
-    rx1, ac1, ry1, sy1, ry2, sx2, rx2, ac2, outv,
-    unit, lsem, ssem, qrecv, arecv, rrecv, krecv, grecv, drecv, urecv, erecv, osem,
+    rx1, ac1, ry1, sy1, ry2, sx2, rx2, ac2, rx3,
+    unit, lsem, ssem, qrecv, arecv, rrecv, krecv, grecv, drecv, urecv, erecv,
 ):
     j = lax.axis_index("blk")
     h = lax.axis_index("head")
@@ -324,9 +324,6 @@
     def add(*terms):
         return functools.reduce(jnp.add, [t.astype(F32) for t in terms])
 
-    def store(cols):
-        pltpu.make_async_copy(outv.at[:, cols], out.at[:, cols], osem.at[0]).start()
-
     def x_start(g):
         first, width = XG[g]
         project(first, first + width)
@@ -357,9 +354,8 @@
         half = width // 2
         landed(ry1[g], erecv.at[0, g, 3])
         one, two = x_sums(g, y)
-        outv[:, first:first + half] = add(one, ry1[g][:, 0:half]).astype(BF)
-        outv[:, first + half:first + width] = add(two, ry1[g][:, half:width]).astype(BF)
-        store(pl.ds(first, width))
+        out[:, first:first + half] = add(one, ry1[g][:, 0:half]).astype(BF)
+        out[:, first + half:first + width] = add(two, ry1[g][:, half:width]).astype(BF)
 
     def y_start(g):
         first, width = YG[g]
@@ -371,7 +367,11 @@
         landed(ry2[g], erecv.at[1, g, 3])
         for i in range(4):
             sx2[g][i] = add(ry2[g][i], pb[i, y, :, first:first + width]).astype(BF)
-        ring_start(1, g, lambda to, cols: sx2[g].at[to, :, cols], rx2[g], 0, width // 2)
+        if g < len(YG) - 1:
+            ring_start(1, g, lambda to, cols: sx2[g].at[to, :, cols], rx2[g], 0, width // 2)
+            return
+        for n, (to, dev) in enumerate(((far, {"head": far * 2 + y}), (up, to_up), (down, to_down))):
+            send(sx2[g].at[to], rx3.at[n], 8, erecv.at[1, g, 2], dev)
 
     def y_pass(g):
         ring_pass(1, g, lambda to, cols: sx2[g][to, :, cols], rx2[g], ac2[g], 0, YG[g][1] // 2)
@@ -379,10 +379,13 @@
     def y_end(g):
         first, width = YG[g]
         half = width // 2
+        if g == len(YG) - 1:
+            landed(rx3, erecv.at[1, g, 2])
+            out[:, first:first + width] = add(sx2[g][x], rx3[0], rx3[1], rx3[2]).astype(BF)
+            return
         landed(rx2[g].at[0:4], erecv.at[1, g, 2])
-        outv[:, first:first + half] = add(sx2[g][x, :, 0:half], rx2[g][4], rx2[g][1]).astype(BF)
-        outv[:, first + half:first + width] = add(sx2[g][x, :, half:width], rx2[g][5], rx2[g][3]).astype(BF)
-        store(pl.ds(first, width))
+        out[:, first:first + half] = add(sx2[g][x, :, 0:half], rx2[g][4], rx2[g][1]).astype(BF)
+        out[:, first + half:first + width] = add(sx2[g][x, :, half:width], rx2[g][5], rx2[g][3]).astype(BF)
 
     x_start(0)
     y_start(0)
@@ -398,14 +401,12 @@
     x_turn(1)
     y_pass(0)
     x_turn(2)
-    y_pass(1)
     x_end(0)
     x_end(1)
     y_end(0)
     x_end(2)
     y_end(1)
 
-    landed(outv, osem.at[0])
     for phase, rows, cols in (
         (0, 32, 4480), (1, 64, 4480), (2, 64, 3840), (3, 128, 5120), (4, 128, 4480), (5, 128, 4480),
         (7, 64, 3840), (8, 256, 4480),
@@ -425,9 +426,9 @@
 
     return pl.pallas_call(
         kernel,
-        out_shape=jax.ShapeDtypeStruct((ROWS, D), BF),
+        out_shape=V((ROWS, D), BF),
         in_specs=[any_spec, vmem, pl.BlockSpec(memory_space=pltpu.SMEM)] + [any_spec] * 5,
-        out_specs=any_spec,
+        out_specs=vmem,
         scratch_shapes=[
             V((3, ROWS, D), BF), V((D // 128, 128), BF), V((D // 128, 128), BF),
             V((L_BLK, GROUP), BF), V((L_BLK, GROUP), BF), V((GROUP, D), BF),
@@ -443,9 +444,9 @@
             [V((ROWS, w), BF) for _, w in XG], [V((ROWS, w), BF) for _, w in XG],
             [V((4, ROWS, w), BF) for _, w in YG], [V((4, ROWS, w), BF) for _, w in YG],
             [V((6, ROWS, w // 2), BF) for _, w in YG], [V((2, ROWS, w // 2), BF) for _, w in YG],
-            V((ROWS, D), BF),
+            V((3, ROWS, YG[-1][1]), BF),
             V((35, 2, CH), F32), dma((8,)), dma((9,)), dma((NP,)), dma((2,)), dma((NP,)), dma((2,)),
-            dma((4, NP)), dma((2, 4, NP)), dma((NP,)), dma((2, 3, 4)), dma((1,)),
+            dma((4, NP)), dma((2, 4, NP)), dma((NP,)), dma((2, 3, 4)),
         ],
         compiler_params=pltpu.CompilerParams(
             collective_id=0, has_side_effects=True, vmem_limit_bytes=56 * 1024 * 1024

time: 80.6 us -> 78.9 us (0.979)
  local copies, waits for them, and re-layouts: 1.72 us -> 0.73 us
    unnamed x1, local copies, waits for them, and re-layouts: 1.72 us -> 0.73 us
where the time goes in v7:
time: 78.9 us; the launch traced here: 78.2 us
  Pallas kernels  77.5 us (98%)
    pallas_call x1, Pallas kernels, local(): pl.pallas_call(kernel, out_shape=V((ROWS, D), BF), in_specs=[any_spec, vm...  77.5 us

profile of v7, /device:TPU:8, one launch (start us, length us, event | category | flops | bytes accessed | tf_op | source)
XLA Modules:
  0.0 78.2 jit_solution(10758125580390591102)
XLA Ops:
  0.0 77.5 %shard_map.82 = bf16[32,5120]{1,0:T(8,128)(2,1)S(1)} custom-call(bf16[3,32,5120]{2,1,0:T(8,128)(2,1)} %bitcast.4, s32[1,256]{1,0:T(1,128)} %bitcast.7, s32[16]{0:T(128)} %counts.1, bf16[512,640]{1,0:T(8,128)(2,1)} %kcache.1, bf16[512,640]{1,0:T(8,128)(2,1)} %vcache.1, bf16[40,128]{1,0:T(8,128)(2,1)} %bitcast.5, bf16[40,128]{1,0:T(8,128)(2,1)} %bitcast.6, ...), custom_call_target="tpu_custom_call" | custom-call | tf_op jit(solution)/shard_map/pallas_call | solution.py:427
  77.5 0.7 copy.10

commit v8 on v7

--- a/solution.py
+++ b/solution.py
@@ -249,12 +249,15 @@
             value = value + ro[way, step, rows, :].astype(F32) * factors[n + 1]
         return value, top, total
 
+    def joins(way, step, p):
+        return drecv.at[p if step == 1 else 25 + p if step == 4 else 5 + 10 * (step - 2) + 5 * way + p]
+
     def give(way, step, p):
         ahead = 5 - step
         slot = ahead if way == 0 else 8 - ahead
         rows = slice(p * HEAD_DIM, (p + 1) * HEAD_DIM)
         if step > (1 if p in LONG[way] else 2):
-            landed(unit.at[0:33], drecv.at[way, step - 2, p])
+            landed(unit.at[0:33], joins(way, step - 1, p))
             value, top, total = joined(slot, p, [(way, step - 2)])
         else:
             value, top, total = of[slot, rows, :], st[slot, p, 0:1], st[slot, p, 1:2]
@@ -263,8 +266,8 @@
         ss[way, step - 1, p, 1:2] = total
         rows = pl.ds(p * HEAD_DIM, HEAD_DIM)
         dev = blk_at(2 if way == 0 else -2)
-        send(ss.at[way, step - 1, p], rs.at[way, step - 1, p], 6, drecv.at[way, step - 1, p], dev)
-        send(so.at[way, step - 1, rows], ro.at[way, step - 1, rows], 5, drecv.at[way, step - 1, p], dev)
+        send(ss.at[way, step - 1, p], rs.at[way, step - 1, p], 6, joins(way, step, p), dev)
+        send(so.at[way, step - 1, rows], ro.at[way, step - 1, rows], 5, joins(way, step, p), dev)
 
     def long_way(p):
         return 0 if p in LONG[0] else 1
@@ -281,10 +284,9 @@
     last_in = sorted(range(NP), key=lambda p: max(order[0].index(p), order[1].index(p)))
 
     for p in last_in:
-        for way in range(2):
-            landed(unit.at[0:33], drecv.at[way, 3, p])
+        landed(unit, joins(0, 4, p))
         value, _, total = joined(0, p, [(0, 3), (1, 3)])
-        abuf[p][...] = (value / total).T.astype(BF)
+        abuf[p][...] = (value * (1.0 / total)).T.astype(BF)
         for first, size, to, offset in ((0, 128, 320, -1), (0, 128, 64, 1), (0, 64, 448, -2), (64, 64, 0, 2)):
             send(abuf[p].at[pl.ds(first, size)], cat[p].at[pl.ds(to, size)], 7, urecv.at[p], blk_at(offset))
         cat[p][192:320] = abuf[p][...]
@@ -412,7 +414,7 @@
         (7, 64, 3840), (8, 256, 4480),
     ):
         landed(wv.at[0:rows, 0:cols], ssem.at[phase])
-    landed(unit, ssem.at[6])
+    landed(unit.at[0:35], ssem.at[6])
 
 
 def local(fresh, rows_index, counts, key_cache, value_cache, q_gain, k_gain, out_weight):
@@ -445,8 +447,8 @@
             [V((4, ROWS, w), BF) for _, w in YG], [V((4, ROWS, w), BF) for _, w in YG],
             [V((6, ROWS, w // 2), BF) for _, w in YG], [V((2, ROWS, w // 2), BF) for _, w in YG],
             V((3, ROWS, YG[-1][1]), BF),
-            V((35, 2, CH), F32), dma((8,)), dma((9,)), dma((NP,)), dma((2,)), dma((NP,)), dma((2,)),
-            dma((4, NP)), dma((2, 4, NP)), dma((NP,)), dma((2, 3, 4)),
+            V((66, 2, CH), F32), dma((8,)), dma((9,)), dma((NP,)), dma((2,)), dma((NP,)), dma((2,)),
+            dma((4, NP)), dma((30,)), dma((NP,)), dma((2, 3, 4)),
         ],
         compiler_params=pltpu.CompilerParams(
             collective_id=0, has_side_effects=True, vmem_limit_bytes=56 * 1024 * 1024

time: 78.9 us -> 78.9 us (level)
  no operation moved by 1% of the time
where the time goes in v8:
time: 78.9 us; the launch traced here: 78.1 us
  Pallas kernels  77.4 us (98%)
    pallas_call x1, Pallas kernels, local(): pl.pallas_call(kernel, out_shape=V((ROWS, D), BF), in_specs=[any_spec, vm...  77.4 us

profile of v8, /device:TPU:8, one launch (start us, length us, event | category | flops | bytes accessed | tf_op | source)
XLA Modules:
  0.0 78.1 jit_solution(15622356705469578601)
XLA Ops:
  0.0 77.4 %shard_map.82 = bf16[32,5120]{1,0:T(8,128)(2,1)S(1)} custom-call(bf16[3,32,5120]{2,1,0:T(8,128)(2,1)} %bitcast.4, s32[1,256]{1,0:T(1,128)} %bitcast.7, s32[16]{0:T(128)} %counts.1, bf16[512,640]{1,0:T(8,128)(2,1)} %kcache.1, bf16[512,640]{1,0:T(8,128)(2,1)} %vcache.1, bf16[40,128]{1,0:T(8,128)(2,1)} %bitcast.5, bf16[40,128]{1,0:T(8,128)(2,1)} %bitcast.6, ...), custom_call_target="tpu_custom_call" | custom-call | tf_op jit(solution)/shard_map/pallas_call | solution.py:429
  77.4 0.7 copy.10

commit v9 on v7

--- a/solution.py
+++ b/solution.py
@@ -259,12 +259,12 @@
         else:
             value, top, total = of[slot, rows, :], st[slot, p, 0:1], st[slot, p, 1:2]
         so[way, step - 1, rows, :] = value.astype(BF)
+        rows = pl.ds(p * HEAD_DIM, HEAD_DIM)
+        dev = blk_at(2 if way == 0 else -2)
+        send(so.at[way, step - 1, rows], ro.at[way, step - 1, rows], 5, drecv.at[way, step - 1, p], dev)
         ss[way, step - 1, p, 0:1] = top
         ss[way, step - 1, p, 1:2] = total
-        rows = pl.ds(p * HEAD_DIM, HEAD_DIM)
-        dev = blk_at(2 if way == 0 else -2)
         send(ss.at[way, step - 1, p], rs.at[way, step - 1, p], 6, drecv.at[way, step - 1, p], dev)
-        send(so.at[way, step - 1, rows], ro.at[way, step - 1, rows], 5, drecv.at[way, step - 1, p], dev)
 
     def long_way(p):
         return 0 if p in LONG[0] else 1

time: 78.9 us -> 79 us (level)
  no operation moved by 1% of the time
where the time goes in v9:
time: 79 us; the launch traced here: 78.2 us
  Pallas kernels  77.5 us (98%)
    pallas_call x1, Pallas kernels, local(): pl.pallas_call(kernel, out_shape=V((ROWS, D), BF), in_specs=[any_spec, vm...  77.5 us

profile of v9, /device:TPU:8, one launch (start us, length us, event | category | flops | bytes accessed | tf_op | source)
XLA Modules:
  0.0 78.2 jit_solution(7807856281244455560)
XLA Ops:
  0.0 77.5 %shard_map.82 = bf16[32,5120]{1,0:T(8,128)(2,1)S(1)} custom-call(bf16[3,32,5120]{2,1,0:T(8,128)(2,1)} %bitcast.4, s32[1,256]{1,0:T(1,128)} %bitcast.7, s32[16]{0:T(128)} %counts.1, bf16[512,640]{1,0:T(8,128)(2,1)} %kcache.1, bf16[512,640]{1,0:T(8,128)(2,1)} %vcache.1, bf16[40,128]{1,0:T(8,128)(2,1)} %bitcast.5, bf16[40,128]{1,0:T(8,128)(2,1)} %bitcast.6, ...), custom_call_target="tpu_custom_call" | custom-call | tf_op jit(solution)/shard_map/pallas_call | solution.py:427
  77.5 0.7 copy.10
